TPU v7x, 256 devices: a whole 4x4x8 slice. The times are simulated.
256 devices in a mesh: row: 8 (over y_hi, x), col: 32 (over y_lo, z, core).
Axes of the slice: x: 4, y: 4 (y_hi: 2, y_lo: 2; y = y_hi * 2 + y_lo), z: 8, core: 2. Of those that a mesh axis runs over, the one named last changes fastest.
Arguments:
- pair_codes: bfloat16 [24, 4096, 128], P('row', 'col'), may hold values from -448 to 448
- exponents: int32 [24, 32], P('row', 'col'), may hold values from -8 to -5
- token_length: int32 [1], replicated, may hold values from 2048 to 4096
- norm_gain: float32 [128], replicated, may hold values from 0.5 to 1.5
- proj_weight: bfloat16 [128, 512], replicated, may hold values from -0.5 to 0.5
- out_weight: bfloat16 [128, 128], replicated, may hold values from -2 to 2
- pair_bias: bfloat16 [4, 4096, 4096], P(None, 'col', 'row'), may hold values from -320 to 320
- update_grad: bfloat16 [24, 4096, 128], P('row', 'col'), may hold values from -6 to 6
Outputs:
- update: bfloat16 [24, 4096, 128], P('row', 'col')
- pair_grad: bfloat16 [24, 4096, 128], P('row', 'col')
- bias_grad: bfloat16 [4, 4096, 4096], P(None, 'col', 'row')
All inputs are finite; a program needn't handle non-finite values.
Results may differ from a plain program's by a relative error of at most 0.029.
Values may be sent and summed in bfloat16 or wider, within the bound.
A program may use at most 128 MiB of HBM per device.

v0:
```python
import math

import jax
import jax.numpy as jnp
from jax import lax
from jax.sharding import PartitionSpec as P

MASKED = -1e30
EPSILON = 1e-05


def key_block(source, offset, count, head_count):
    key_rows = lax.dynamic_slice_in_dim(source[0], offset, count, 1)
    value_rows = lax.dynamic_slice_in_dim(source[1], offset, count, 1)
    row_count, span, inner_width = key_rows.shape
    head_size = inner_width // head_count
    return (
        key_rows.reshape(row_count, span, head_count, head_size),
        value_rows.reshape(row_count, span, head_count, head_size),
    )


def scores_of(query_heads, key_heads, bias_block, valid):
    scores = jnp.einsum(
        "rqhd,rkhd->rqhk", query_heads, key_heads, preferred_element_type=jnp.float32
    )
    scores = scores + bias_block[None].astype(jnp.float32)
    return jnp.where(valid, scores, MASKED)


def shards(
    pair_codes, exponents, token_length, norm_gain, proj_weight, out_weight, pair_bias, update_grad
):
    row_count, col_width, channels = pair_codes.shape
    head_count = pair_bias.shape[0]
    inner_width = out_weight.shape[0]
    head_size = inner_width // head_count
    qscale = head_size ** (-0.5)
    total_keys = col_width * lax.axis_size("col")
    live_keys = token_length[0]
    tile_scale = jnp.exp2(exponents.astype(jnp.float32))
    pair_values = pair_codes.astype(jnp.float32) * tile_scale[:, :, None]
    average = jnp.mean(pair_values, axis=-1, keepdims=True)
    centered = pair_values - average
    variance = jnp.mean(centered * centered, axis=-1, keepdims=True)
    inv_std = lax.rsqrt(variance + EPSILON)
    unit_pair = centered * inv_std
    normed = (unit_pair * norm_gain).astype(jnp.bfloat16)
    projected = jnp.dot(
        normed.reshape(row_count * col_width, channels),
        proj_weight,
        preferred_element_type=jnp.float32,
    )
    projected = projected.reshape(row_count, col_width, 4 * inner_width)
    queries = (projected[..., :inner_width] * qscale).astype(jnp.bfloat16)
    own_keys = projected[..., inner_width : 2 * inner_width].astype(jnp.bfloat16)
    own_values = projected[..., 2 * inner_width : 3 * inner_width].astype(jnp.bfloat16)
    gates = jax.nn.sigmoid(projected[..., 3 * inner_width :])
    query_heads = queries.reshape(row_count, col_width, head_count, head_size)
    full_bias = lax.all_gather(pair_bias, "row", axis=2, tiled=True)
    bias_turned = jnp.transpose(full_bias, (1, 0, 2))
    start_state = (
        jnp.full((row_count, col_width, head_count), MASKED, jnp.float32),
        jnp.zeros((row_count, col_width, head_count), jnp.float32),
        jnp.zeros((row_count, col_width, head_count, head_size), jnp.float32),
    )
    source = (
        lax.all_gather(own_keys, "col", axis=1, tiled=True),
        lax.all_gather(own_values, "col", axis=1, tiled=True),
    )
    piece_width = source[0].shape[1]
    step_keys = math.gcd(piece_width, 512)

    def one_block(block_number, carry):
        running_max, running_sum, weighted = carry
        offset = block_number * step_keys
        key_heads, value_heads = key_block(source, offset, step_keys, head_count)
        bias_block = lax.dynamic_slice_in_dim(bias_turned, offset, step_keys, 2)
        valid = offset + jnp.arange(step_keys, dtype=jnp.int32) < live_keys
        scores = scores_of(query_heads, key_heads, bias_block, valid)
        new_max = jnp.maximum(running_max, jnp.max(scores, axis=-1))
        rescale = jnp.exp(running_max - new_max)
        weights = jnp.exp(scores - new_max[..., None])
        running_sum = running_sum * rescale + jnp.sum(weights, axis=-1)
        weighted = weighted * rescale[..., None] + jnp.einsum(
            "rqhk,rkhd->rqhd",
            weights.astype(jnp.bfloat16),
            value_heads,
            preferred_element_type=jnp.float32,
        )
        return (new_max, running_sum, weighted)

    final_state = lax.fori_loop(0, piece_width // step_keys, one_block, start_state)
    running_max, running_sum, weighted = final_state
    log_total = running_max + jnp.log(running_sum)
    attended = (weighted / running_sum[..., None]).reshape(row_count, col_width, inner_width)
    gated = (gates * attended).astype(jnp.bfloat16)
    update = jnp.dot(
        gated.reshape(row_count * col_width, inner_width),
        out_weight,
        preferred_element_type=jnp.float32,
    )
    update = update.reshape(row_count, col_width, channels).astype(jnp.bfloat16)
    d_gated = jnp.dot(
        update_grad.reshape(row_count * col_width, channels),
        out_weight.T,
        preferred_element_type=jnp.float32,
    )
    d_gated = d_gated.reshape(row_count, col_width, inner_width)
    d_gate_pre = d_gated * attended * gates * (1.0 - gates)
    d_attended = (d_gated * gates).astype(jnp.bfloat16)
    delta = jnp.sum(
        (d_attended.astype(jnp.float32) * attended).reshape(
            row_count, col_width, head_count, head_size
        ),
        axis=-1,
    )
    d_heads = d_attended.reshape(row_count, col_width, head_count, head_size)
    gathered = (
        lax.all_gather(own_keys, "col", axis=1, tiled=True),
        lax.all_gather(own_values, "col", axis=1, tiled=True),
    )
    weight_f = proj_weight.astype(jnp.float32)
    highest = lax.Precision.HIGHEST
    w_key_t = weight_f[:, inner_width : 2 * inner_width].T
    w_value_t = weight_f[:, 2 * inner_width : 3 * inner_width].T
    step_all = math.gcd(total_keys, 512)

    def block_terms(key_heads, value_heads, bias_block, valid, d_query_sum):
        scores = scores_of(query_heads, key_heads, bias_block, valid)
        probs = jnp.exp(scores - log_total[..., None])
        d_probs = jnp.einsum(
            "rqhd,rkhd->rqhk", d_heads, value_heads, preferred_element_type=jnp.float32
        )
        d_scores = probs * (d_probs - delta[..., None])
        d_scores_b = d_scores.astype(jnp.bfloat16)
        d_query_sum = d_query_sum + jnp.einsum(
            "rqhk,rkhd->rqhd", d_scores_b, key_heads, preferred_element_type=jnp.float32
        )
        d_keys = jnp.einsum(
            "rqhk,rqhd->rkhd", d_scores_b, query_heads, preferred_element_type=jnp.float32
        )
        d_values = jnp.einsum(
            "rqhk,rqhd->rkhd",
            probs.astype(jnp.bfloat16),
            d_heads,
            preferred_element_type=jnp.float32,
        )
        span = key_heads.shape[1]
        key_term = jnp.dot(
            d_keys.reshape(row_count * span, inner_width), w_key_t, precision=highest
        )
        key_term = key_term + jnp.dot(
            d_values.reshape(row_count * span, inner_width), w_value_t, precision=highest
        )
        bias_term = jnp.transpose(jnp.sum(d_scores, axis=0), (1, 0, 2))
        return (d_query_sum, key_term.reshape(row_count, span, channels), bias_term)

    d_query_start = jnp.zeros((row_count, col_width, head_count, head_size), jnp.float32)
    key_start = jnp.zeros((row_count, total_keys, channels), jnp.float32)

    def back_block(block_number, carry):
        d_query_sum, key_buffer, bias_buffer = carry
        offset = block_number * step_all
        key_heads, value_heads = key_block(gathered, offset, step_all, head_count)
        bias_block = lax.dynamic_slice_in_dim(bias_turned, offset, step_all, 2)
        valid = offset + jnp.arange(step_all, dtype=jnp.int32) < live_keys
        d_query_sum, key_term, bias_term = block_terms(
            key_heads, value_heads, bias_block, valid, d_query_sum
        )
        key_buffer = lax.dynamic_update_slice_in_dim(key_buffer, key_term, offset, 1)
        bias_buffer = lax.dynamic_update_slice_in_dim(bias_buffer, bias_term, offset, 2)
        return (d_query_sum, key_buffer, bias_buffer)

    bias_start = jnp.zeros((head_count, col_width, total_keys), jnp.float32)
    d_query_sum, key_buffer, bias_buffer = lax.fori_loop(
        0, total_keys // step_all, back_block, (d_query_start, key_start, bias_start)
    )
    bias_grad = lax.psum_scatter(
        bias_buffer.astype(jnp.bfloat16), "row", scatter_dimension=2, tiled=True
    )
    key_grad = lax.psum_scatter(
        key_buffer.astype(jnp.bfloat16), "col", scatter_dimension=1, tiled=True
    ).astype(jnp.float32)
    d_queries = d_query_sum.reshape(row_count * col_width, inner_width) * qscale
    d_normed = jnp.dot(d_queries, weight_f[:, :inner_width].T, precision=highest)
    d_normed = d_normed + jnp.dot(
        d_gate_pre.reshape(row_count * col_width, inner_width),
        weight_f[:, 3 * inner_width :].T,
        precision=highest,
    )
    d_normed = d_normed.reshape(row_count, col_width, channels) + key_grad
    scaled = d_normed * norm_gain
    pair_grad = inv_std * (
        scaled
        - jnp.mean(scaled, axis=-1, keepdims=True)
        - unit_pair * jnp.mean(scaled * unit_pair, axis=-1, keepdims=True)
    )
    return (update, pair_grad.astype(jnp.bfloat16), bias_grad)


def solution(mesh):
    in_specs = (
        P("row", "col", None),
        P("row", "col"),
        P(),
        P(),
        P(),
        P(),
        P(None, "col", "row"),
        P("row", "col", None),
    )
    out_specs = (P("row", "col", None), P("row", "col", None), P(None, "col", "row"))
    return jax.shard_map(shards, mesh=mesh, in_specs=in_specs, out_specs=out_specs, check_vma=False)
```

profile of v0, /device:TPU:1, one launch (start us, length us, event | category | flops | bytes accessed | tf_op | source)
XLA Modules:
  0.0 660.8 jit_solution(14144534537880946812)
XLA Ops:
  13.1 2.0 copy.55
  16.3 66.5 %all-gather.4.cloned.1.call-done = bf16[3,4096,128]{2,1,0:T(8,128)(2,1)} async-done(((bf16[3,128,128]{2,1,0:T(8,128)(2,1)}), bf16[3,4096,128]{2,1,0:T(8,128)(2,1)}) %all-gather.4.cloned.1.call-update) | async-done | bytes 3145744 | tf_op jit(solution)/shard_map/all_gather | solution.py:68
  82.8 4.7 copy.56
  87.5 63.4 %all-gather.8.cloned.1.call-done = bf16[3,4096,128]{2,1,0:T(8,128)(2,1)} async-done(((bf16[3,128,128]{2,1,0:T(8,128)(2,1)}), bf16[3,4096,128]{2,1,0:T(8,128)(2,1)}) %all-gather.8.cloned.1.call-update) | async-done | bytes 3145744 | tf_op jit(solution)/shard_map/all_gather | solution.py:69
  151.0 4.7 copy.57
  155.7 74.0 %all-gather.6.cloned.1.call-done = bf16[4,128,4096]{1,2,0:T(8,128)(2,1)} async-done(((bf16[4,128,512]{1,2,0:T(8,128)(2,1)}), bf16[4,128,4096]{1,2,0:T(8,128)(2,1)}) %all-gather.6.cloned.1.call-update) | async-done | bytes 4194320 | tf_op jit(solution)/shard_map/all_gather | solution.py:60
  229.6 63.3 %while.36 = (s32[]{:T(128)}, f32[3,128,4]{1,2,0:T(4,128)S(1)}, f32[3,128,4]{1,2,0:T(4,128)}, f32[3,128,4,32]{1,3,2,0:T(8,128)S(1)}, s32[]{:T(128)}, /*index=5*/b...) while((s32[]{:T(128)}, f32[3,128,4]{1,2,0:T(4,128)S(1)}, ...), condition=%wide.region_5.6_spmd.clone, body=%wide.region_2.5_spmd.clone.sunk | while | flops 109732352 | bytes 27122064 | solution.py:93
  231.5 1.9 constant_dynamic-slice_fusion.6
  234.4 2.0 fusion.108
  239.4 1.9 constant_dynamic-slice_fusion.6
  242.3 2.0 fusion.108
  247.3 1.9 constant_dynamic-slice_fusion.6
  250.2 2.0 fusion.108
  255.2 1.9 constant_dynamic-slice_fusion.6
  258.1 2.0 fusion.108
  263.1 1.9 constant_dynamic-slice_fusion.6
  266.0 2.0 fusion.108
  271.0 1.9 constant_dynamic-slice_fusion.6
  274.0 2.0 fusion.108
  278.9 1.9 constant_dynamic-slice_fusion.6
  281.9 2.0 fusion.108
  286.8 1.9 constant_dynamic-slice_fusion.6
  289.8 2.0 fusion.108
  294.5 1.8 convert_multiply_fusion
  296.6 2.0 broadcast_in_dim.70
  298.7 2.5 broadcast_in_dim.71.clone
  301.2 144.4 %while.37 = (s32[]{:T(128)}, f32[3,128,4,32]{1,3,2,0:T(8,128)}, bf16[3,4096,128]{2,1,0:T(8,128)(2,1)}, bf16[4,128,4096]{2,1,0:T(8,128)(2,1)}, bf16[3,4096,128]{1...) while((s32[]{:T(128)}, f32[3,128,4,32]{1,3,2,0:T(8,128)}, ...), condition=%wide.region_9.10_spmd.clone, body=%wide.region_7.9_spmd.clone.sunk | while | flops 864781312 | bytes 54939556 | solution.py:176
  305.0 3.5 fusion.126
  308.5 2.7 fusion.127
  315.9 1.4 convolution_add_fusion.3
  323.0 3.5 fusion.126
  326.5 2.7 fusion.127
  341.0 3.5 fusion.126
  344.5 2.7 fusion.127
  359.1 3.5 fusion.126
  362.6 2.7 fusion.127
  377.2 3.5 fusion.126
  380.7 2.7 fusion.127
  395.3 3.5 fusion.126
  398.8 2.7 fusion.127
  413.3 3.5 fusion.126
  416.8 2.7 fusion.127
  431.3 3.5 fusion.126
  434.8 2.7 fusion.127
  447.1 1.8 convolution_convert_fusion
  449.1 111.7 %reduce-scatter.3.cloned.1.call-done = bf16[3,128,128]{2,1,0:T(8,128)(2,1)} async-done(((bf16[3,4096,128]{2,1,0:T(8,128)(2,1)}), bf16[3,128,128]{2,1,0:T(8,128)(2,1)}) %reduce-scatter.3.cloned.1.call-update) | async-done | bytes 98320 | tf_op jit(solution)/shard_map/reduce_scatter | solution.py:182
  562.0 1.8 multiply_convert_fusion
  563.8 90.5 %reduce-scatter.5.cloned.1.call-done = bf16[4,128,512]{2,1,0:T(8,128)(2,1)} async-done(((bf16[4,128,4096]{2,1,0:T(8,128)(2,1)}), bf16[4,128,512]{2,1,0:T(8,128)(2,1)}) %reduce-scatter.5.cloned.1.call-update) | async-done | bytes 524304 | tf_op jit(solution)/shard_map/reduce_scatter | solution.py:179
  (457 shorter events, 134.4 us)
Async XLA Ops:
  7.2 287.3 %copy-start = (bf16[3,128,128]{2,1,0:T(8,128)(2,1)S(1)}, bf16[3,128,128]{2,1,0:T(8,128)(2,1)}, u32[]{:S(2)}) copy-start(bf16[3,128,128]{2,1,0:T(8,128)(2,1)} %param.19) | copy-start | bytes 294916
  7.2 8.1 %copy-start.14 = (bf16[128,512]{1,0:T(8,128)(2,1)S(1)}, bf16[128,512]{1,0:T(8,128)(2,1)}, u32[]{:S(2)}) copy-start(bf16[128,512]{1,0:T(8,128)(2,1)} %param.16) | copy-start | bytes 393220
  7.2 75.6 %all-gather.4.cloned.1.call-start = ((), (), s32[]{:S(2)}) async-start(), calls=%async_computation.2 | async-start | bytes 3244032 | tf_op jit(solution)/shard_map/all_gather | solution.py:68
  7.9 7.5 %copy-start.27 = (f32[3]{0:T(128)}, f32[3]{0:T(128)S(1)}, u32[]{:S(2)}) copy-start(f32[3]{0:T(128)S(1)} %exponential_bitcast_fusion) | copy-start | bytes 40
  9.1 6.4 copy-start.23
  10.2 5.2 copy-start.25
  11.5 76.0 %copy-start.13 = (f32[3,128,512]{2,1,0:T(8,128)}, f32[3,128,512]{2,1,0:T(8,128)S(1)}, u32[]{:S(2)}) copy-start(f32[3,128,512]{2,1,0:T(8,128)S(1)} %get-tuple-element.606) | copy-start | bytes 2359300
  12.3 138.7 %all-gather.8.cloned.1.call-start = ((), (), s32[]{:S(2)}) async-start(), calls=%async_computation.4 | async-start | bytes 3244032 | tf_op jit(solution)/shard_map/all_gather | solution.py:69
  13.1 216.6 %all-gather.6.cloned.1.call-start = ((), (), s32[]{:S(2)}) async-start(), calls=%async_computation.3 | async-start | bytes 4718592 | tf_op jit(solution)/shard_map/all_gather | solution.py:60
  15.2 545.6 %reduce-scatter.3.cloned.1.call-start = ((), (), s32[]{:S(2)}) async-start(), calls=%async_computation.5 | async-start | bytes 3244032 | tf_op jit(solution)/shard_map/reduce_scatter | solution.py:182
  231.4 2.9 copy-start.21
  239.4 2.9 copy-start.21
  247.3 2.9 copy-start.21
  255.2 2.9 copy-start.21
  263.1 2.9 copy-start.21
  271.0 2.9 copy-start.21
  278.9 2.9 copy-start.21
  286.8 2.9 copy-start.21
  293.8 7.5 %copy-start.19 = (f32[3,128,128]{2,1,0:T(8,128)}, f32[3,128,128]{2,1,0:T(8,128)S(1)}, u32[]{:S(2)}) copy-start(f32[3,128,128]{2,1,0:T(8,128)S(1)} %copy.58) | copy-start | bytes 589828
  296.6 4.6 copy-start.11
  303.7 4.8 copy-start.4
  308.5 2.7 copy-start.3
  315.1 3.1 copy-start.7
  321.7 4.8 copy-start.4
  326.5 2.7 copy-start.3
  333.1 3.1 copy-start.7
  339.7 4.8 copy-start.4
  351.1 3.1 copy-start.7
  357.7 4.8 copy-start.4
  362.6 2.7 copy-start.3
  369.1 3.1 copy-start.7
  375.8 4.8 copy-start.4
  387.2 3.1 copy-start.7
  393.9 4.8 copy-start.4
  398.8 2.7 copy-start.3
  405.3 3.1 copy-start.7
  412.0 4.8 copy-start.4
  423.4 3.1 copy-start.7
  430.0 4.8 copy-start.4
  434.8 2.7 copy-start.3
  441.4 3.1 copy-start.7
  445.6 208.6 %reduce-scatter.5.cloned.1.call-start = ((), (), s32[]{:S(2)}) async-start(), calls=%async_computation.6 | async-start | bytes 4718592 | tf_op jit(solution)/shard_map/reduce_scatter | solution.py:179
  445.7 3.1 copy-start.18
  445.7 115.1 %copy-start.10 = (bf16[3,128,128]{2,1,0:T(8,128)(2,1)S(1)}, bf16[3,128,128]{2,1,0:T(8,128)(2,1)}, u32[]{:S(2)}) copy-start(bf16[3,128,128]{2,1,0:T(8,128)(2,1)} %param.12) | copy-start | bytes 294916
  445.7 115.1 %copy-start.24 = (f32[3,128]{1,0:T(4,128)S(1)}, f32[3,128]{1,0:T(4,128)}, u32[]{:S(2)}) copy-start(f32[3,128]{1,0:T(4,128)} %copy-done.23) | copy-start | bytes 4612
  445.7 115.0 %copy-start.26 = (f32[3,128]{1,0:T(4,128)S(1)}, f32[3,128]{1,0:T(4,128)}, u32[]{:S(2)}) copy-start(f32[3,128]{1,0:T(4,128)} %copy-done.25) | copy-start | bytes 4612
  445.7 115.0 %copy-start.28 = (f32[3]{0:T(128)S(1)}, f32[3]{0:T(128)}, u32[]{:S(2)}) copy-start(f32[3]{0:T(128)} %copy-done.27) | copy-start | bytes 40
  445.7 115.0 %copy-start.29 = (f32[128]{0:T(128)S(1)}, f32[128]{0:T(128)}, u32[]{:S(2)}) copy-start(f32[128]{0:T(128)} %param.15) | copy-start | bytes 1540
  (79 other events, 150.4 us)
Sparse Core Ops, SparseCore 0:
  12.4 70.2 all-gather.3
  85.2 65.7 all-gather.7
  154.2 75.4 all-gather.5
  445.7 114.9 reduce-scatter.2
  565.9 88.2 reduce-scatter.4
where the time goes:
time: 663 us; the launch traced here: 661 us
  waiting for transfers between devices  407 us (61%)
  matrix products  111 us (17%)
  local copies, waits for them, and re-layouts  72.3 us (11%)
  other arithmetic  53.7 us (8%)
  between operations  14.1 us (2%)
    reduce_scatter x1, waiting for transfers between devices, shards(): lax.psum_scatter(key_buffer.astype(jnp.bfloat16), 'col', scatter_dimensio...  112 us
    reduce_scatter x1, waiting for transfers between devices, shards(): lax.psum_scatter(bias_buffer.astype(jnp.bfloat16), 'row', scatter_dimensi...  90.5 us
    all_gather x1, waiting for transfers between devices, shards(): full_bias = lax.all_gather(pair_bias, 'row', axis=2, tiled=True)  74 us
    all_gather x1, waiting for transfers between devices, shards(): lax.all_gather(own_keys, 'col', axis=1, tiled=True)  66.5 us
    all_gather x1, waiting for transfers between devices, shards(): lax.all_gather(own_values, 'col', axis=1, tiled=True)  63.4 us
    dot_general x8, matrix products, block_terms(): jnp.einsum('rqhd,rkhd->rqhk', d_heads, value_heads, preferred_element_typ...  27.9 us
    dynamic_slice x16, local copies, waits for them, and re-layouts, key_block(): value_rows = lax.dynamic_slice_in_dim(source[1], offset, count, 1)  24.7 us
    dot_general x8, matrix products, block_terms(): jnp.einsum('rqhk,rkhd->rqhd', d_scores_b, key_heads, preferred_element_ty...  21.5 us
  transfers between devices with their start and end apart: 5, of which 5 were waited for; matrix products, arithmetic and copies ran while one was open for 3% of the time, Pallas kernels for 0%

commit v1 on v0

v1 whole, which is shorter than its diff:
```python
import functools

import jax
import jax.numpy as jnp
from jax import lax
from jax.experimental import pallas as pl
from jax.experimental.pallas import tpu as pltpu
from jax.sharding import PartitionSpec as P

MASKED = -1e30
EPSILON = 1e-05
F32 = jnp.float32
BF = jnp.bfloat16
NX, NZ = 4, 8
HEADS, DH, C, T = 4, 32, 128, 128
KB = 512
ROWS = 3


def nn(a, b):
    return lax.dot_general(a, b, (((1,), (0,)), ((), ())), preferred_element_type=F32)


def nt(a, b):
    return lax.dot_general(a, b, (((1,), (1,)), ((), ())), preferred_element_type=F32)


def split_nn(w, a):
    high = a.astype(BF)
    low = (a - high.astype(F32)).astype(BF)
    return nn(w, high) + nn(w, low)


def per_head(stat):
    return jnp.concatenate(
        [jnp.broadcast_to(stat[h : h + 1, :], (DH, T)) for h in range(HEADS)], axis=0
    )


def kernel(
    tok, codes, expo, gain, w, wo, bias, ug,
    update, pair_grad, bias_grad,
    wt, wot, nb, unit, inv, gates, dgated, kn, qt, dot, bias_g, bias_t, probs, s_ref, qbd, dos,
    m_st, l_st, a_st, vals, keys_t, gk, att_loc, st_loc, att_tx, att_rx, st_rx, back_tx, back_rx, stats, dgp,
    ds_ref, acc, dq, kt, rxc, ytx, rxy, rsum, ztx, zrx, ftx, frx, dqtx, dqrx, gtx, grx,
    bx_s, bx_r, ks_s, ks_r, zr_s, zr_r, sb_s, sb_r, pq_s, pq_r, ex_s, ex_r, kc_s, kc_r,
    ky_s, ky_r, zq_s, zq_r, f_s, f_r, g_s, g_r,
):
    row_id = lax.axis_index("row")
    col_id = lax.axis_index("col")
    yh, x = row_id // NX, lax.rem(row_id, NX)
    yl, z, c = col_id // 16, lax.rem(col_id, 16) // 2, lax.rem(col_id, 2)
    xs = [lax.rem(x + i, NX) for i in range(NX)]
    zs = [lax.rem(z + i, NZ) for i in range(NZ)]

    def dev(x_=x, yh_=yh, yl_=yl, z_=z, c_=c):
        return (yh_ * NX + x_, yl_ * 16 + z_ * 2 + c_)

    def rc(src, dst, send, recv, to):
        return pltpu.make_async_remote_copy(
            src_ref=src, dst_ref=dst, send_sem=send, recv_sem=recv,
            device_id=to, device_id_type=pl.DeviceIdType.MESH,
        )

    xp, xm, zp, zm = dev(x_=xs[1]), dev(x_=xs[3]), dev(z_=zs[1]), dev(z_=zs[7])
    sib = dev(c_=1 - c)
    ypart = dev(yl_=1 - yl)
    hpart = dev(yh_=1 - yh)
    cross = dev(yh_=1 - yh, yl_=1 - yl)
    swap = dev(yh_=yl, yl_=yh)
    is_home = yh == yl

    barrier = pltpu.get_barrier_semaphore()
    for to in (xp, xm, zp, zm, sib, ypart, hpart, cross):
        pl.semaphore_signal(barrier, inc=1, device_id=to, device_id_type=pl.DeviceIdType.MESH)
    pl.semaphore_wait(barrier, 8)

    bias_p = rc(bias, bias_g.at[0], bx_s.at[0], bx_r.at[0], xp)
    bias_m = rc(bias, bias_g.at[1], bx_s.at[1], bx_r.at[1], xm)
    bias_fp = rc(bias_g.at[0, pl.ds(0, 2)], bias_g.at[2, pl.ds(0, 2)], bx_s.at[2], bx_r.at[2], xp)
    bias_fm = rc(bias_g.at[1, pl.ds(2, 2)], bias_g.at[2, pl.ds(2, 2)], bx_s.at[3], bx_r.at[3], xm)
    bias_p.start()
    bias_m.start()

    gain_row = gain[...]
    for r in range(ROWS):
        scale = jnp.exp2(expo[r : r + 1, 0:1].astype(F32))
        value = codes[r].astype(F32) * scale
        mean = jnp.mean(value, axis=-1, keepdims=True)
        centered = value - mean
        var = jnp.mean(centered * centered, axis=-1, keepdims=True)
        inv_std = lax.rsqrt(var + EPSILON)
        unit_pair = centered * inv_std
        unit[r] = unit_pair
        inv[r] = jnp.broadcast_to(inv_std, (T, C))
        nb[r] = (unit_pair * gain_row).astype(BF)

    def key_at(zz, cc):
        return pl.ds(pl.multiple_of(zz * 256 + cc * 128, 128), 128)

    my_set = pl.ds(pl.multiple_of(yh * ROWS, ROWS), ROWS)
    key_send = [
        rc(nb, kn.at[pl.ds(yh * ROWS, ROWS), key_at(z, c)], ks_s.at[t], ks_r.at[yh], dev(yh_=yl, yl_=t))
        for t in range(2)
    ]
    for t in range(2):
        @pl.when(jnp.logical_not(jnp.logical_and(is_home, yl == t)))
        def _():
            key_send[t].start()

    @pl.when(is_home)
    def _():
        kn[pl.ds(yh * ROWS, ROWS), key_at(z, c), :] = nb[...]

    for q in range(4):
        wt[q * 128 : (q + 1) * 128, :] = w[:, q * 128 : (q + 1) * 128].astype(F32).T.astype(BF)
    wot[...] = wo[...].astype(F32).T.astype(BF)

    def set_of(ref, s):
        return ref.at[pl.ds(s * ROWS, ROWS)]

    for r in range(ROWS):
        n = nb[r]
        qt[yh * ROWS + r] = (nt(wt[0:128, :], n) * (DH ** -0.5)).astype(BF)
        gate = jax.nn.sigmoid(nt(wt[384:512, :], n))
        gates[r] = gate
        dg = nt(wo[...], ug[r])
        dgated[r] = dg
        dot[yh * ROWS + r] = (dg * gate).astype(BF)
    q_send = rc(set_of(qt, yh), set_of(qt, yh), pq_s.at[0], pq_r.at[0], hpart)
    d_send = rc(set_of(dot, yh), set_of(dot, yh), pq_s.at[1], pq_r.at[1], hpart)
    q_send.start()
    d_send.start()

    live = tok[0]

    def prep(src, xb):
        for k in range(4):
            first = (yh * NX + xb) * KB + k * 128
            valid = first + lax.broadcasted_iota(jnp.int32, (128, 128), 0) < live
            for h in range(HEADS):
                tile = src[h, :, k * 128 : (k + 1) * 128].astype(F32).T
                bias_t[xb, k * 128 : (k + 1) * 128, h * 128 : (h + 1) * 128] = jnp.where(valid, tile, MASKED)

    qbd[...] = jnp.zeros_like(qbd)
    dos[...] = jnp.zeros_like(dos)
    prep(bias, x)

    for s in range(2):
        @pl.when(jnp.logical_not(jnp.logical_and(is_home, yh == s)))
        def _():
            rc(nb, kn.at[pl.ds(s * ROWS, ROWS), key_at(z, c)], ks_s.at[0], ks_r.at[s], sib).wait_recv()

    def block(zz, cc=c):
        return kn.at[:, key_at(zz, cc)]

    def half(zz, s):
        return kn.at[pl.ds(s * ROWS, ROWS), key_at(zz, c)]

    def up(i):
        src = block(zs[(8 - i) % 8]) if i < 3 else half(zs[5], 0)
        return rc(src, src, zr_s.at[0, i], zr_r.at[0, i], zp)

    def down(i):
        src = block(zs[i]) if i < 3 else half(zs[3], 1)
        return rc(src, src, zr_s.at[1, i], zr_r.at[1, i], zm)

    def to_sib(i):
        return rc(block(zs[i]), block(zs[i]), sb_s.at[i], sb_r.at[i], sib)

    def from_sib(i):
        return rc(block(zs[i], 1 - c), block(zs[i], 1 - c), sb_s.at[i], sb_r.at[i], sib)

    def up_in(i):
        dst = block(zs[7 - i]) if i < 3 else half(zs[4], 0)
        return rc(dst, dst, zr_s.at[0, i], zr_r.at[0, i], zp)

    def down_in(i):
        dst = block(zs[i + 1]) if i < 3 else half(zs[4], 1)
        return rc(dst, dst, zr_s.at[1, i], zr_r.at[1, i], zm)

    def ring_step(i):
        up_in(i).wait_recv()
        if i < 3:
            up(i + 1).start()
            to_sib(7 - i).start()
        down_in(i).wait_recv()
        if i < 3:
            down(i + 1).start()
            to_sib(i + 1).start()
        else:
            to_sib(4).start()

    up(0).start()
    down(0).start()
    to_sib(0).start()
    bias_p.wait_recv()
    bias_fp.start()
    bias_m.wait_recv()
    bias_fm.start()
    prep(bias_g.at[0], xs[3])
    prep(bias_g.at[1], xs[1])
    ring_step(0)
    rc(set_of(qt, yh), set_of(qt, 1 - yh), pq_s.at[0], pq_r.at[0], hpart).wait_recv()

    zb = z // 2
    even = lax.rem(z, 2) == 0
    near = jnp.where(even, zb + 3, zb + 1)
    far = jnp.where(even, zb + 1, zb + 3)

    def arrive(phase):
        for i in ((0, 1, 7), (2, 6), (3, 5), (4,))[phase]:
            from_sib(i).wait_recv()

    ones = jnp.ones((16, KB), BF)

    def load_q(row):
        for h in range(HEADS):
            qbd[h * 32 : (h + 1) * 32, h * 128 : (h + 1) * 128] = qt[row, h * 32 : (h + 1) * 32, :]

    att_copy = rc(att_tx, att_rx, ex_s.at[0], ex_r.at[0], hpart)
    st_copy = rc(set_of(st_loc, 1 - yh), st_rx, ex_s.at[1], ex_r.at[1], hpart)
    back_copy = rc(back_tx, back_rx, ex_s.at[2], ex_r.at[2], hpart)

    def combine(row):
        m_all = [m_st[row * 4 + i] for i in range(4)]
        top_m = jnp.maximum(jnp.maximum(m_all[0], m_all[1]), jnp.maximum(m_all[2], m_all[3]))
        total = jnp.zeros((HEADS, T), F32)
        weighted = jnp.zeros((C, T), F32)
        for i in range(4):
            f = jnp.exp(m_all[i] - top_m)
            total = total + f * l_st[row * 4 + i]
            weighted = weighted + per_head(f) * a_st[row * 4 + i]
        st_loc[row, 0:4, :] = top_m
        st_loc[row, 4:8, :] = total
        return weighted

    def forward(u, carry):
        phase, t = u // 6, lax.rem(u, 6)
        row = lax.rem((1 - yh) * ROWS + t, 2 * ROWS)
        xb = lax.rem(
            jnp.where(phase == 0, zb, jnp.where(phase == 1, near, jnp.where(phase == 2, far, zb + 2))), NX
        )
        slot = row * 4 + xb

        for i in range(4):
            @pl.when(u == 6 * i)
            def _():
                arrive(i)

        @pl.when(jnp.logical_and(t == 0, xb == xs[2]))
        def _():
            bias_fp.wait_recv()
            bias_fm.wait_recv()
            prep(bias_g.at[2], xs[2])

        for i in range(1, 4):
            @pl.when(u == 6 * i - 3)
            def _():
                ring_step(i)

        load_q(row)

        @pl.when(u < 6)
        def _():
            gk[row] = nn(w[:, 128:256], qbd[...]).astype(BF)

        n = kn[row, pl.ds(pl.multiple_of(xb * KB, KB), KB), :]
        kv = nn(n, w[:, 128:384]).astype(BF)
        kvt = nt(wt[128:384, :], n).astype(BF)
        k = kv[:, 0:128]
        vals[slot] = kv[:, 128:256]
        keys_t[slot] = kvt[0:128, :]
        vt = kvt[128:256, :]
        for hp in range(2):
            cols = slice(hp * 256, hp * 256 + 256)
            q2 = qbd[:, cols]
            top = None
            for i in range(4):
                rows = slice(i * 128, (i + 1) * 128)
                s = nn(k[rows, :], q2) + bias_t[xb, rows, cols]
                s_ref[rows, cols] = s
                part = jnp.max(s.reshape(16, 8, 256), axis=0)
                top = part if top is None else jnp.maximum(top, part)
            m = jnp.max(top, axis=0, keepdims=True)
            for i in range(4):
                rows = slice(i * 128, (i + 1) * 128)
                probs[slot, rows, cols] = jnp.exp(s_ref[rows, cols] - m).astype(BF)
            a = nn(jnp.concatenate([vt[hp * 64 : hp * 64 + 64, :], ones], axis=0), probs[slot, :, cols])
            for j in range(2):
                h = hp * 2 + j
                lanes = slice(j * 128, (j + 1) * 128)
                m_st[slot, h : h + 1, :] = m[:, lanes]
                l_st[slot, h : h + 1, :] = a[64:65, lanes]
                a_st[slot, h * 32 : (h + 1) * 32, :] = a[j * 32 : (j + 1) * 32, lanes]

        @pl.when(u == 20)
        def _():
            for r in range(ROWS):
                att_tx[r] = combine((1 - yh) * ROWS + r).astype(BF)
            att_copy.start()
            st_copy.start()

        return carry

    lax.fori_loop(0, 24, forward, 0)

    for r in range(ROWS):
        att_loc[yh * ROWS + r] = combine(yh * ROWS + r)
    att_copy.wait_recv()
    st_copy.wait_recv()
    for r in range(ROWS):
        mine = yh * ROWS + r
        ma, la = st_loc[mine, 0:4, :], st_loc[mine, 4:8, :]
        mb, lb = st_rx[r, 0:4, :], st_rx[r, 4:8, :]
        top_m = jnp.maximum(ma, mb)
        fa, fb = jnp.exp(ma - top_m), jnp.exp(mb - top_m)
        total = fa * la + fb * lb
        attended = (per_head(fa) * att_loc[mine] + per_head(fb) * att_rx[r].astype(F32)) / per_head(total)
        gate = gates[r]
        product = dot[mine].astype(F32) * attended
        lse = top_m + jnp.log(total)
        stats[mine, 0:4, :] = lse
        back_tx[r, 0:4, :] = lse
        for h in range(HEADS):
            delta = jnp.sum(product[h * 32 : (h + 1) * 32, :], axis=0, keepdims=True)
            stats[mine, 4 + h : 5 + h, :] = delta
            back_tx[r, 4 + h : 5 + h, :] = delta
        att_loc[mine] = attended
    back_copy.start()
    for r in range(ROWS):
        attended = att_loc[yh * ROWS + r]
        gate = gates[r]
        dgp[r] = dgated[r] * attended * gate * (1.0 - gate)
        update[r] = nn(wot[...], (gate * attended).astype(BF)).T.astype(BF)
    rc(set_of(dot, yh), set_of(dot, 1 - yh), pq_s.at[1], pq_r.at[1], hpart).wait_recv()
    dq[...] = jnp.zeros_like(dq)

    order = [xs[2], xs[1], xs[3], xs[0]]

    def core_copy(zz):
        return rc(kt.at[:, key_at(zz, 1 - c)], rxc.at[zz], kc_s.at[zz], kc_r.at[zz], sib)

    def y_copy(zz):
        return rc(ytx.at[zz], rxy.at[zz], ky_s.at[zz], ky_r.at[zz], ypart)

    def core_stage(xb):
        for b in range(2):
            core_copy(xb * 2 + b).start()

    def y_stage(xb):
        for b in range(2):
            zz = xb * 2 + b
            core_copy(zz).wait_recv()
            for r in range(ROWS):
                theirs, ours = (1 - yl) * ROWS + r, yl * ROWS + r
                ytx[zz, r] = (kt[theirs, key_at(zz, c), :].astype(F32) + rxc[zz, theirs].astype(F32)).astype(BF)
                rsum[zz, r] = kt[ours, key_at(zz, c), :].astype(F32) + rxc[zz, ours].astype(F32)
            y_copy(zz).start()

    def sum_stage(xb):
        for b in range(2):
            zz = xb * 2 + b
            y_copy(zz).wait_recv()
            rsum[zz] = rsum[zz] + rxy[zz].astype(F32)

    g_half_p = rc(gtx.at[0, pl.ds(0, 2)], grx.at[0, pl.ds(0, 2)], g_s.at[0], g_r.at[0], xp)
    g_half_m = rc(gtx.at[0, pl.ds(2, 2)], grx.at[0, pl.ds(2, 2)], g_s.at[1], g_r.at[1], xm)
    g_p = rc(gtx.at[1], grx.at[1], g_s.at[2], g_r.at[2], xp)
    g_m = rc(gtx.at[2], grx.at[2], g_s.at[3], g_r.at[3], xm)

    def turned(h, k):
        return acc[k * 128 : (k + 1) * 128, h * 128 : (h + 1) * 128].T

    def bias_stage(step):
        if step == 1:
            g_half_p.wait_recv()
        if step == 2:
            g_half_m.wait_recv()
        if step == 3:
            g_p.wait_recv()
            g_m.wait_recv()
        for h in range(HEADS):
            for k in range(4):
                lanes = slice(k * 128, (k + 1) * 128)
                tile = turned(h, k)
                if (step == 1 and h < 2) or (step == 2 and h >= 2):
                    tile = tile + grx[0, h, :, lanes].astype(F32)
                if step == 3:
                    tile = tile + grx[1, h, :, lanes].astype(F32) + grx[2, h, :, lanes].astype(F32)
                    bias_grad[h, :, lanes] = tile.astype(BF)
                else:
                    gtx[step, h, :, lanes] = tile.astype(BF)
        if step == 0:
            g_half_p.start()
            g_half_m.start()
        if step == 1:
            g_p.start()
        if step == 2:
            g_m.start()

    def backward(u, carry):
        step = u // 6
        xb = lax.rem(x + jnp.where(step == 0, 2, jnp.where(step == 1, 1, jnp.where(step == 2, 3, 0))), NX)
        row = lax.rem(yh * ROWS + lax.rem(u, 6), 2 * ROWS)
        slot = row * 4 + xb

        @pl.when(u == 3)
        def _():
            back_copy.wait_recv()
            for r in range(ROWS):
                stats[(1 - yh) * ROWS + r] = back_rx[r]

        @pl.when(lax.rem(u, 6) == 0)
        def _():
            acc[...] = jnp.zeros_like(acc)

        st = stats[row]
        f = jnp.exp(m_st[slot] - st[0:4, :])
        dls = f * st[4:8, :]
        for h in range(HEADS):
            rows = slice(h * 32, (h + 1) * 32)
            dos[rows, h * 128 : (h + 1) * 128] = (dot[row, rows, :].astype(F32) * f[h : h + 1, :]).astype(BF)
        keys = pl.ds(pl.multiple_of(xb * KB, KB), KB)
        v = vals[slot]
        key_t = keys_t[slot]
        for hp in range(2):
            cols = slice(hp * 256, hp * 256 + 256)
            d2 = dos[:, cols]
            l2 = jnp.concatenate([dls[hp * 2 : hp * 2 + 1, :], dls[hp * 2 + 1 : hp * 2 + 2, :]], axis=1)
            for i in range(4):
                rows = slice(i * 128, (i + 1) * 128)
                d_prob = nn(v[rows, :], d2) - l2
                d_score = probs[slot, rows, cols].astype(F32) * d_prob
                acc[rows, cols] = acc[rows, cols] + d_score
                ds_ref[rows, cols] = d_score.astype(BF)
            d_query = nn(key_t[hp * 64 : hp * 64 + 64, :], ds_ref[:, cols])
            for j in range(2):
                rows = slice((hp * 2 + j) * 32, (hp * 2 + j + 1) * 32)
                dq[row, rows, :] = dq[row, rows, :] + d_query[j * 32 : (j + 1) * 32, j * 128 : (j + 1) * 128]
        gv = nn(w[:, 256:384], dos[...]).astype(BF)
        kt[row, keys, :] = (nt(ds_ref[...], gk[row]) + nt(probs[slot], gv)).astype(BF)

        for s in range(4):
            @pl.when(u == 6 * s + 5)
            def _():
                bias_stage(s) if s < 3 else None
                core_stage(order[s])
                if s >= 1:
                    y_stage(order[s - 1])
                if s >= 2:
                    sum_stage(order[s - 2])

        return carry

    lax.fori_loop(0, 24, backward, 0)

    for r in range(ROWS):
        dqtx[r] = dq[(1 - yh) * ROWS + r].astype(BF)
    dq_copy = rc(dqtx, dqrx, f_s.at[0], f_r.at[0], hpart)
    dq_copy.start()
    y_stage(order[3])
    sum_stage(order[2])
    sum_stage(order[3])

    def z_copy(way, i):
        if i == 0:
            part = pl.ds(way * 64, 64)
            src, dst = ztx.at[way, 0, :, part], zrx.at[way, 0, :, part]
        else:
            src, dst = ztx.at[way, i], zrx.at[way, i]
        return rc(src, dst, zq_s.at[way, i], zq_r.at[way, i], zp if way == 0 else zm)

    for i in range(4):
        for way in range(2):
            home = zs[(4 - i) if way == 0 else (4 + i)]
            if i == 0:
                part = slice(way * 64, way * 64 + 64)
                ztx[way, 0, :, part, :] = rsum[home, :, part, :].astype(BF)
            else:
                z_copy(way, i - 1).wait_recv()
                if i == 1:
                    part = slice(way * 64, way * 64 + 64)
                    other = slice(64 - way * 64, 128 - way * 64)
                    ztx[way, 1, :, part, :] = (
                        rsum[home, :, part, :] + zrx[way, 0, :, part, :].astype(F32)
                    ).astype(BF)
                    ztx[way, 1, :, other, :] = rsum[home, :, other, :].astype(BF)
                else:
                    ztx[way, i] = (rsum[home] + zrx[way, i - 1].astype(F32)).astype(BF)
            z_copy(way, i).start()
    bias_stage(3)
    z_copy(0, 3).wait_recv()
    z_copy(1, 3).wait_recv()
    ftx[...] = (rsum[z] + zrx[0, 3].astype(F32) + zrx[1, 3].astype(F32)).astype(BF)
    final = rc(ftx, frx, f_s.at[1], f_r.at[1], swap)

    @pl.when(jnp.logical_not(is_home))
    def _():
        final.start()

    @pl.when(is_home)
    def _():
        frx[...] = ftx[...]

    dq_copy.wait_recv()
    for r in range(ROWS):
        d_query = (dq[yh * ROWS + r] + dqrx[r].astype(F32)) * (DH ** -0.5)
        unit_t = split_nn(w[:, 0:128], d_query) + split_nn(w[:, 384:512], dgp[r])
        dgated[r] = unit_t.T

    @pl.when(jnp.logical_not(is_home))
    def _():
        final.wait_recv()

    for r in range(ROWS):
        d_normed = dgated[r] + frx[r].astype(F32)
        e = d_normed * gain_row
        up_r = unit[r]
        pair_grad[r] = (
            inv[r]
            * (e - jnp.mean(e, axis=-1, keepdims=True) - up_r * jnp.mean(e * up_r, axis=-1, keepdims=True))
        ).astype(BF)

    for copy in (bias_p, bias_m, bias_fp, bias_fm, q_send, d_send, att_copy, st_copy, back_copy, dq_copy,
                 g_half_p, g_half_m, g_p, g_m):
        copy.wait_send()
    for t in range(2):
        @pl.when(jnp.logical_not(jnp.logical_and(is_home, yl == t)))
        def _():
            key_send[t].wait_send()
    for i in range(4):
        up(i).wait_send()
        down(i).wait_send()
        z_copy(0, i).wait_send()
        z_copy(1, i).wait_send()
    for i in range(8):
        to_sib(i).wait_send()
        core_copy(zs[i]).wait_send()
        y_copy(zs[i]).wait_send()

    @pl.when(jnp.logical_not(is_home))
    def _():
        final.wait_send()


def shards(codes, expo, tok, gain, w, wo, bias, ug):
    vm = pltpu.VMEM
    dma = pltpu.SemaphoreType.DMA
    blk = (ROWS, T, C)
    scratch = [
        vm((512, C), BF), vm((C, C), BF), vm(blk, BF), vm(blk, F32), vm(blk, F32), vm(blk, F32), vm(blk, F32),
        vm((6, 2048, C), BF), vm((6, C, T), BF), vm((6, C, T), BF), vm((3, HEADS, T, KB), BF),
        vm((4, KB, 512), F32), vm((24, KB, 512), BF), vm((KB, 512), F32), vm((C, 512), BF), vm((C, 512), BF),
        vm((24, HEADS, T), F32), vm((24, HEADS, T), F32), vm((24, C, T), F32),
        vm((24, KB, C), BF), vm((24, C, KB), BF), vm((6, C, 512), BF), vm((6, C, T), F32), vm((6, 8, T), F32),
        vm(blk, BF), vm(blk, BF), vm((ROWS, 8, T), F32), vm((ROWS, 8, T), F32), vm((ROWS, 8, T), F32),
        vm((6, 8, T), F32), vm(blk, F32),
        vm((KB, 512), BF), vm((KB, 512), F32), vm((6, C, T), F32), vm((6, 2048, C), BF),
        vm((8, 6, T, C), BF), vm((8, 3, T, C), BF), vm((8, 3, T, C), BF), vm((8, 3, T, C), F32),
        vm((2, 4, 3, T, C), BF), vm((2, 4, 3, T, C), BF), vm(blk, BF), vm(blk, BF), vm(blk, BF), vm(blk, BF),
        vm((3, HEADS, T, KB), BF), vm((3, HEADS, T, KB), BF),
        dma((4,)), dma((4,)), dma((2,)), dma((2,)), dma((2, 4)), dma((2, 4)), dma((8,)), dma((8,)),
        dma((2,)), dma((2,)), dma((3,)), dma((3,)), dma((8,)), dma((8,)), dma((8,)), dma((8,)),
        dma((2, 4)), dma((2, 4)), dma((2,)), dma((2,)), dma((4,)), dma((4,)),
    ]
    v = pl.BlockSpec(memory_space=pltpu.VMEM)
    return pl.pallas_call(
        kernel,
        out_shape=(
            jax.ShapeDtypeStruct(blk, BF),
            jax.ShapeDtypeStruct(blk, BF),
            jax.ShapeDtypeStruct((HEADS, T, KB), BF),
        ),
        in_specs=[pl.BlockSpec(memory_space=pltpu.SMEM)] + [v] * 7,
        out_specs=(v, v, v),
        scratch_shapes=scratch,
        compiler_params=pltpu.CompilerParams(
            collective_id=0, has_side_effects=True, vmem_limit_bytes=58 * 1024 * 1024
        ),
        cost_estimate=pl.CostEstimate(flops=8_000_000_000, bytes_accessed=4_000_000, transcendentals=6_300_000),
    )(tok, codes, expo, gain.reshape(1, C), w, wo, bias, ug)


def solution(mesh):
    in_specs = (
        P("row", "col", None), P("row", "col"), P(), P(), P(), P(), P(None, "col", "row"), P("row", "col", None),
    )
    out_specs = (P("row", "col", None), P("row", "col", None), P(None, "col", "row"))
    return jax.shard_map(shards, mesh=mesh, in_specs=in_specs, out_specs=out_specs, check_vma=False)
```

time: 663 us -> 122 us (0.18)
  the two profiles are of different devices: /device:TPU:1 before, /device:TPU:8 now
where the time goes in v1:
time: 122 us
  Pallas kernels  115 us (94%)
  local copies, waits for them, and re-layouts  5.4 us (4%)
  between operations  1.3 us (1%)
    pallas_call x1, Pallas kernels, shards(): pl.pallas_call(kernel, out_shape=(jax.ShapeDtypeStruct(blk, BF), jax.Shap...  115 us
    unnamed x8, local copies, waits for them, and re-layouts  5.4 us

profile of v1, /device:TPU:8, one launch (start us, length us, event | category | flops | bytes accessed | tf_op | source)
XLA Modules:
  0.0 122.2 jit_solution(1908899524411741053)
XLA Ops:
  1.3 0.0 copy-start.1
  1.3 0.6 copy-done.1
  1.9 0.7 copy.11.expo
  2.6 115.5 %shard_map.103 = (bf16[3,128,128]{2,1,0:T(8,128)(2,1)}, bf16[3,128,128]{2,1,0:T(8,128)(2,1)}, bf16[4,128,512]{2,1,0:T(8,128)(2,1)}) custom-call(s32[1]{0:T(128)S(6)} %copy.15.tok, bf16[3,128,128]{2,1,0:T(8,128)(2,1)} %codes.1, s32[3,1]{1,0:T(4,128)} %copy.11.expo, f32[1,128]{1,0:T(1,128)} %bitcast.1, bf16[128,512]{1,0:T(8,128)(2,1)} %w.1, ...), custom_call_target="tpu_custom_call" | custom-call | flops 8000000000 | bytes 4000000 | tf_op jit(solution)/shard_map/pallas_call | solution.py:568
  118.1 0.0 copy-start
  118.1 1.6 %copy.16 = bf16[3,128,128]{2,1,0:T(8,128)(2,1)} copy(bf16[3,128,128]{2,1,0:T(8,128)(2,1)} %get-tuple-element.6) | data formatting | bytes 196608
  119.7 0.0 copy-done
  119.7 0.6 copy.17
  120.3 1.9 %copy.18 = bf16[4,128,512]{2,1,0:T(8,128)(2,1)} copy(bf16[4,128,512]{2,1,0:T(8,128)(2,1)} %get-tuple-element.8) | data formatting | bytes 1048576
Async XLA Ops:
  1.3 0.7 copy-start.1
  118.1 1.6 %copy-start = (bf16[3,128,128]{2,1,0:T(8,128)(2,1)S(1)}, bf16[3,128,128]{2,1,0:T(8,128)(2,1)}, u32[]{:S(2)}) copy-start(bf16[3,128,128]{2,1,0:T(8,128)(2,1)} %get-tuple-element.7) | copy-start | bytes 294916

commit v2 on v1

--- a/solution.py
+++ b/solution.py
@@ -1,5 +1,3 @@
-import functools
-
 import jax
 import jax.numpy as jnp
 from jax import lax
@@ -37,14 +35,34 @@
     )
 
 
+def normalised(codes, expo, r):
+    value = codes[r].astype(F32) * jnp.exp2(expo[0:1, r : r + 1].astype(F32))
+    centered = value - jnp.mean(value, axis=-1, keepdims=True)
+    inv_std = lax.rsqrt(jnp.mean(centered * centered, axis=-1, keepdims=True) + EPSILON)
+    return centered * inv_std, inv_std
+
+
+def norm_back(codes, expo, gain, d_normed, update_in, bias_in, update, pair_grad, bias_grad):
+    update[...] = update_in[...]
+    bias_grad[...] = bias_in[...]
+    for r in range(ROWS):
+        unit, inv_std = normalised(codes, expo, r)
+        e = d_normed[r] * gain[...]
+        pair_grad[r] = (
+            inv_std
+            * (e - jnp.mean(e, axis=-1, keepdims=True) - unit * jnp.mean(e * unit, axis=-1, keepdims=True))
+        ).astype(BF)
+
+
 def kernel(
     tok, codes, expo, gain, w, wo, bias, ug,
-    update, pair_grad, bias_grad,
-    wt, wot, nb, unit, inv, gates, dgated, kn, qt, dot, bias_g, bias_t, probs, s_ref, qbd, dos,
+    update_hbm, normed_hbm, bias_hbm,
+    update, bias_grad,
+    wt, wot, nb, gates, dgated, kn, qt, dot, bias_g, bias_t, probs, s_ref, qbd, dos,
     m_st, l_st, a_st, vals, keys_t, gk, att_loc, st_loc, att_tx, att_rx, st_rx, back_tx, back_rx, stats, dgp,
-    ds_ref, acc, dq, kt, rxc, ytx, rxy, rsum, ztx, zrx, ftx, frx, dqtx, dqrx, gtx, grx,
+    ds_ref, k_ref, vt_ref, gv_ref, acc, dq, kt, rxc, ytx, rxy, rsum, ztx, zrx, ftx, frx, dqtx, dqrx, gtx, grx,
     bx_s, bx_r, ks_s, ks_r, zr_s, zr_r, sb_s, sb_r, pq_s, pq_r, ex_s, ex_r, kc_s, kc_r,
-    ky_s, ky_r, zq_s, zq_r, f_s, f_r, g_s, g_r,
+    ky_s, ky_r, zq_s, zq_r, f_s, f_r, g_s, g_r, o_s,
 ):
     row_id = lax.axis_index("row")
     col_id = lax.axis_index("col")
@@ -73,6 +91,11 @@
     barrier = pltpu.get_barrier_semaphore()
     for to in (xp, xm, zp, zm, sib, ypart, hpart, cross):
         pl.semaphore_signal(barrier, inc=1, device_id=to, device_id_type=pl.DeviceIdType.MESH)
+
+    gain_row = gain[...]
+    for r in range(ROWS):
+        nb[r] = (normalised(codes, expo, r)[0] * gain_row).astype(BF)
+
     pl.semaphore_wait(barrier, 8)
 
     bias_p = rc(bias, bias_g.at[0], bx_s.at[0], bx_r.at[0], xp)
@@ -81,19 +104,6 @@
     bias_fm = rc(bias_g.at[1, pl.ds(2, 2)], bias_g.at[2, pl.ds(2, 2)], bx_s.at[3], bx_r.at[3], xm)
     bias_p.start()
     bias_m.start()
-
-    gain_row = gain[...]
-    for r in range(ROWS):
-        scale = jnp.exp2(expo[r : r + 1, 0:1].astype(F32))
-        value = codes[r].astype(F32) * scale
-        mean = jnp.mean(value, axis=-1, keepdims=True)
-        centered = value - mean
-        var = jnp.mean(centered * centered, axis=-1, keepdims=True)
-        inv_std = lax.rsqrt(var + EPSILON)
-        unit_pair = centered * inv_std
-        unit[r] = unit_pair
-        inv[r] = jnp.broadcast_to(inv_std, (T, C))
-        nb[r] = (unit_pair * gain_row).astype(BF)
 
     def key_at(zz, cc):
         return pl.ds(pl.multiple_of(zz * 256 + cc * 128, 128), 128)
@@ -130,9 +140,8 @@
     q_send = rc(set_of(qt, yh), set_of(qt, yh), pq_s.at[0], pq_r.at[0], hpart)
     d_send = rc(set_of(dot, yh), set_of(dot, yh), pq_s.at[1], pq_r.at[1], hpart)
     q_send.start()
-    d_send.start()
-
-    live = tok[0]
+
+    live = tok[...].reshape(1, 1)
 
     def prep(src, xb):
         for k in range(4):
@@ -201,7 +210,6 @@
     prep(bias_g.at[0], xs[3])
     prep(bias_g.at[1], xs[1])
     ring_step(0)
-    rc(set_of(qt, yh), set_of(qt, 1 - yh), pq_s.at[0], pq_r.at[0], hpart).wait_recv()
 
     zb = z // 2
     even = lax.rem(z, 2) == 0
@@ -212,7 +220,8 @@
         for i in ((0, 1, 7), (2, 6), (3, 5), (4,))[phase]:
             from_sib(i).wait_recv()
 
-    ones = jnp.ones((16, KB), BF)
+    vt_ref[64:80, :] = jnp.ones((16, KB), BF)
+    vt_ref[144:160, :] = jnp.ones((16, KB), BF)
 
     def load_q(row):
         for h in range(HEADS):
@@ -237,7 +246,7 @@
 
     def forward(u, carry):
         phase, t = u // 6, lax.rem(u, 6)
-        row = lax.rem((1 - yh) * ROWS + t, 2 * ROWS)
+        row = lax.rem(jnp.where(phase == 3, 1 - yh, yh) * ROWS + t, 2 * ROWS)
         xb = lax.rem(
             jnp.where(phase == 0, zb, jnp.where(phase == 1, near, jnp.where(phase == 2, far, zb + 2))), NX
         )
@@ -259,6 +268,11 @@
             def _():
                 ring_step(i)
 
+        @pl.when(u == 3)
+        def _():
+            rc(set_of(qt, yh), set_of(qt, 1 - yh), pq_s.at[0], pq_r.at[0], hpart).wait_recv()
+            d_send.start()
+
         load_q(row)
 
         @pl.when(u < 6)
@@ -266,19 +280,23 @@
             gk[row] = nn(w[:, 128:256], qbd[...]).astype(BF)
 
         n = kn[row, pl.ds(pl.multiple_of(xb * KB, KB), KB), :]
-        kv = nn(n, w[:, 128:384]).astype(BF)
-        kvt = nt(wt[128:384, :], n).astype(BF)
-        k = kv[:, 0:128]
-        vals[slot] = kv[:, 128:256]
-        keys_t[slot] = kvt[0:128, :]
-        vt = kvt[128:256, :]
+        for i in range(4):
+            rows = slice(i * 128, (i + 1) * 128)
+            kv = nn(n[rows, :], w[:, 128:384]).astype(BF)
+            k_ref[rows, :] = kv[:, 0:128]
+            vals[slot, rows, :] = kv[:, 128:256]
+        for i in range(2):
+            lanes = slice(i * 256, (i + 1) * 256)
+            keys_t[slot, :, lanes] = nt(wt[128:256, :], n[lanes, :]).astype(BF)
+            vt_ref[0:64, lanes] = nt(wt[256:320, :], n[lanes, :]).astype(BF)
+            vt_ref[80:144, lanes] = nt(wt[320:384, :], n[lanes, :]).astype(BF)
         for hp in range(2):
             cols = slice(hp * 256, hp * 256 + 256)
             q2 = qbd[:, cols]
             top = None
             for i in range(4):
                 rows = slice(i * 128, (i + 1) * 128)
-                s = nn(k[rows, :], q2) + bias_t[xb, rows, cols]
+                s = nn(k_ref[rows, :], q2) + bias_t[xb, rows, cols]
                 s_ref[rows, cols] = s
                 part = jnp.max(s.reshape(16, 8, 256), axis=0)
                 top = part if top is None else jnp.maximum(top, part)
@@ -286,7 +304,7 @@
             for i in range(4):
                 rows = slice(i * 128, (i + 1) * 128)
                 probs[slot, rows, cols] = jnp.exp(s_ref[rows, cols] - m).astype(BF)
-            a = nn(jnp.concatenate([vt[hp * 64 : hp * 64 + 64, :], ones], axis=0), probs[slot, :, cols])
+            a = nn(vt_ref[hp * 80 : hp * 80 + 80, :], probs[slot, :, cols])
             for j in range(2):
                 h = hp * 2 + j
                 lanes = slice(j * 128, (j + 1) * 128)
@@ -333,6 +351,8 @@
         gate = gates[r]
         dgp[r] = dgated[r] * attended * gate * (1.0 - gate)
         update[r] = nn(wot[...], (gate * attended).astype(BF)).T.astype(BF)
+    update_out = pltpu.make_async_copy(update, update_hbm, o_s.at[0])
+    update_out.start()
     rc(set_of(dot, yh), set_of(dot, 1 - yh), pq_s.at[1], pq_r.at[1], hpart).wait_recv()
     dq[...] = jnp.zeros_like(dq)
 
@@ -421,8 +441,6 @@
         for h in range(HEADS):
             rows = slice(h * 32, (h + 1) * 32)
             dos[rows, h * 128 : (h + 1) * 128] = (dot[row, rows, :].astype(F32) * f[h : h + 1, :]).astype(BF)
-        keys = pl.ds(pl.multiple_of(xb * KB, KB), KB)
-        v = vals[slot]
         key_t = keys_t[slot]
         for hp in range(2):
             cols = slice(hp * 256, hp * 256 + 256)
@@ -430,16 +448,20 @@
             l2 = jnp.concatenate([dls[hp * 2 : hp * 2 + 1, :], dls[hp * 2 + 1 : hp * 2 + 2, :]], axis=1)
             for i in range(4):
                 rows = slice(i * 128, (i + 1) * 128)
-                d_prob = nn(v[rows, :], d2) - l2
-                d_score = probs[slot, rows, cols].astype(F32) * d_prob
+                d_score = probs[slot, rows, cols].astype(F32) * (nn(vals[slot, rows, :], d2) - l2)
                 acc[rows, cols] = acc[rows, cols] + d_score
                 ds_ref[rows, cols] = d_score.astype(BF)
             d_query = nn(key_t[hp * 64 : hp * 64 + 64, :], ds_ref[:, cols])
             for j in range(2):
                 rows = slice((hp * 2 + j) * 32, (hp * 2 + j + 1) * 32)
                 dq[row, rows, :] = dq[row, rows, :] + d_query[j * 32 : (j + 1) * 32, j * 128 : (j + 1) * 128]
-        gv = nn(w[:, 256:384], dos[...]).astype(BF)
-        kt[row, keys, :] = (nt(ds_ref[...], gk[row]) + nt(probs[slot], gv)).astype(BF)
+        for i in range(2):
+            lanes = slice(i * 256, (i + 1) * 256)
+            gv_ref[:, lanes] = nn(w[:, 256:384], dos[:, lanes]).astype(BF)
+        for i in range(4):
+            rows = slice(i * 128, (i + 1) * 128)
+            term = nt(ds_ref[rows, :], gk[row]) + nt(probs[slot, rows, :], gv_ref[...])
+            kt[row, pl.ds(pl.multiple_of(xb * KB + i * 128, 128), 128), :] = term.astype(BF)
 
         for s in range(4):
             @pl.when(u == 6 * s + 5)
@@ -490,6 +512,8 @@
                     ztx[way, i] = (rsum[home] + zrx[way, i - 1].astype(F32)).astype(BF)
             z_copy(way, i).start()
     bias_stage(3)
+    bias_out = pltpu.make_async_copy(bias_grad, bias_hbm, o_s.at[1])
+    bias_out.start()
     z_copy(0, 3).wait_recv()
     z_copy(1, 3).wait_recv()
     ftx[...] = (rsum[z] + zrx[0, 3].astype(F32) + zrx[1, 3].astype(F32)).astype(BF)
@@ -514,13 +538,9 @@
         final.wait_recv()
 
     for r in range(ROWS):
-        d_normed = dgated[r] + frx[r].astype(F32)
-        e = d_normed * gain_row
-        up_r = unit[r]
-        pair_grad[r] = (
-            inv[r]
-            * (e - jnp.mean(e, axis=-1, keepdims=True) - up_r * jnp.mean(e * up_r, axis=-1, keepdims=True))
-        ).astype(BF)
+        dgated[r] = dgated[r] + frx[r].astype(F32)
+    normed_out = pltpu.make_async_copy(dgated, normed_hbm, o_s.at[2])
+    normed_out.start()
 
     for copy in (bias_p, bias_m, bias_fp, bias_fm, q_send, d_send, att_copy, st_copy, back_copy, dq_copy,
                  g_half_p, g_half_m, g_p, g_m):
@@ -543,43 +563,58 @@
     def _():
         final.wait_send()
 
+    update_out.wait()
+    bias_out.wait()
+    normed_out.wait()
+
 
 def shards(codes, expo, tok, gain, w, wo, bias, ug):
     vm = pltpu.VMEM
     dma = pltpu.SemaphoreType.DMA
     blk = (ROWS, T, C)
     scratch = [
-        vm((512, C), BF), vm((C, C), BF), vm(blk, BF), vm(blk, F32), vm(blk, F32), vm(blk, F32), vm(blk, F32),
+        vm(blk, BF), vm((HEADS, T, KB), BF),
+        vm((512, C), BF), vm((C, C), BF), vm(blk, BF), vm(blk, F32), vm(blk, F32),
         vm((6, 2048, C), BF), vm((6, C, T), BF), vm((6, C, T), BF), vm((3, HEADS, T, KB), BF),
         vm((4, KB, 512), F32), vm((24, KB, 512), BF), vm((KB, 512), F32), vm((C, 512), BF), vm((C, 512), BF),
         vm((24, HEADS, T), F32), vm((24, HEADS, T), F32), vm((24, C, T), F32),
         vm((24, KB, C), BF), vm((24, C, KB), BF), vm((6, C, 512), BF), vm((6, C, T), F32), vm((6, 8, T), F32),
         vm(blk, BF), vm(blk, BF), vm((ROWS, 8, T), F32), vm((ROWS, 8, T), F32), vm((ROWS, 8, T), F32),
         vm((6, 8, T), F32), vm(blk, F32),
-        vm((KB, 512), BF), vm((KB, 512), F32), vm((6, C, T), F32), vm((6, 2048, C), BF),
+        vm((KB, 512), BF), vm((KB, C), BF), vm((160, KB), BF), vm((C, 512), BF), vm((KB, 512), F32), vm((6, C, T), F32), vm((6, 2048, C), BF),
         vm((8, 6, T, C), BF), vm((8, 3, T, C), BF), vm((8, 3, T, C), BF), vm((8, 3, T, C), F32),
         vm((2, 4, 3, T, C), BF), vm((2, 4, 3, T, C), BF), vm(blk, BF), vm(blk, BF), vm(blk, BF), vm(blk, BF),
         vm((3, HEADS, T, KB), BF), vm((3, HEADS, T, KB), BF),
         dma((4,)), dma((4,)), dma((2,)), dma((2,)), dma((2, 4)), dma((2, 4)), dma((8,)), dma((8,)),
         dma((2,)), dma((2,)), dma((3,)), dma((3,)), dma((8,)), dma((8,)), dma((8,)), dma((8,)),
-        dma((2, 4)), dma((2, 4)), dma((2,)), dma((2,)), dma((4,)), dma((4,)),
+        dma((2, 4)), dma((2, 4)), dma((2,)), dma((2,)), dma((4,)), dma((4,)), dma((3,)),
     ]
     v = pl.BlockSpec(memory_space=pltpu.VMEM)
-    return pl.pallas_call(
+    hbm = pl.BlockSpec(memory_space=pl.ANY)
+    shapes = (
+        jax.ShapeDtypeStruct(blk, BF),
+        jax.ShapeDtypeStruct(blk, F32),
+        jax.ShapeDtypeStruct((HEADS, T, KB), BF),
+    )
+    gain, expo = gain.reshape(1, C), expo.reshape(1, ROWS)
+    update, d_normed, bias_grad = pl.pallas_call(
         kernel,
-        out_shape=(
-            jax.ShapeDtypeStruct(blk, BF),
-            jax.ShapeDtypeStruct(blk, BF),
-            jax.ShapeDtypeStruct((HEADS, T, KB), BF),
-        ),
-        in_specs=[pl.BlockSpec(memory_space=pltpu.SMEM)] + [v] * 7,
-        out_specs=(v, v, v),
+        out_shape=shapes,
+        in_specs=[v] * 8,
+        out_specs=(hbm, hbm, hbm),
         scratch_shapes=scratch,
         compiler_params=pltpu.CompilerParams(
             collective_id=0, has_side_effects=True, vmem_limit_bytes=58 * 1024 * 1024
         ),
         cost_estimate=pl.CostEstimate(flops=8_000_000_000, bytes_accessed=4_000_000, transcendentals=6_300_000),
-    )(tok, codes, expo, gain.reshape(1, C), w, wo, bias, ug)
+    )(tok, codes, expo, gain, w, wo, bias, ug)
+    return pl.pallas_call(
+        norm_back,
+        out_shape=(shapes[0], shapes[0], shapes[2]),
+        in_specs=[v] * 6,
+        out_specs=(v, v, v),
+        compiler_params=pltpu.CompilerParams(vmem_limit_bytes=58 * 1024 * 1024),
+    )(codes, expo, gain, d_normed, update, bias_grad)
 
 
 def solution(mesh):

time: 122 us -> 120 us (0.984)
  local copies, waits for them, and re-layouts: 5.4 us -> 0 us
  Pallas kernels: 115 us -> 119 us
    unnamed x8 -> x0, local copies, waits for them, and re-layouts: 5.4 us -> none
    pallas_call x1 -> x2, Pallas kernels: 115 us -> 119 us  [the longest x1 116 us: shards(): pl.pallas_call(kernel, out_shape=shapes, in_specs=[v] * 8, out_specs=(hbm...]
where the time goes in v2:
time: 120 us
  Pallas kernels  119 us (99%)
  between operations  1.28 us (1%)
    pallas_call x1, Pallas kernels, shards(): pl.pallas_call(kernel, out_shape=shapes, in_specs=[v] * 8, out_specs=(hbm...  116 us
    pallas_call x1, Pallas kernels, shards(): pl.pallas_call(norm_back, out_shape=(shapes[0], shapes[0], shapes[2]), in...  2.53 us

profile of v2, /device:TPU:8, one launch (start us, length us, event | category | flops | bytes accessed | tf_op | source)
XLA Modules:
  0.0 119.9 jit_solution(5891802000935372267)
XLA Ops:
  1.3 116.1 %shard_map.103 = (bf16[3,128,128]{2,1,0:T(8,128)(2,1)}, f32[3,128,128]{2,1,0:T(8,128)}, bf16[4,128,512]{2,1,0:T(8,128)(2,1)}) custom-call(s32[1]{0:T(128)S(6)} %copy.11.tok, bf16[3,128,128]{2,1,0:T(8,128)(2,1)} %codes.3, s32[1,3]{1,0:T(1,128)} %bitcast.2, f32[1,128]{1,0:T(1,128)} %bitcast.4, bf16[128,512]{1,0:T(8,128)(2,1)} %w.1, bf16[128,128]{1,0:T(8,128)(2,1)} %wo.1, ...), custom_call_target="tpu_custom_call" | custom-call | flops 8000000000 | bytes 4000000 | tf_op jit(solution)/shard_map/pallas_call | solution.py:600
  117.3 2.5 %shard_map.104 = (bf16[3,128,128]{2,1,0:T(8,128)(2,1)}, bf16[3,128,128]{2,1,0:T(8,128)(2,1)}, bf16[4,128,512]{2,1,0:T(8,128)(2,1)}) custom-call(bf16[3,128,128]{2,1,0:T(8,128)(2,1)} %codes.3, s32[1,3]{1,0:T(1,128)} %bitcast.3, f32[1,128]{1,0:T(1,128)} %bitcast.5, f32[3,128,128]{2,1,0:T(8,128)} %get-tuple-element.6.d_normed, ...), custom_call_target="tpu_custom_call" | custom-call | tf_op jit(solution)/shard_map/pallas_call | solution.py:611

commit v3 on v2

--- a/solution.py
+++ b/solution.py
@@ -60,7 +60,7 @@
     update, bias_grad,
     wt, wot, nb, gates, dgated, kn, qt, dot, bias_g, bias_t, probs, s_ref, qbd, dos,
     m_st, l_st, a_st, vals, keys_t, gk, att_loc, st_loc, att_tx, att_rx, st_rx, back_tx, back_rx, stats, dgp,
-    ds_ref, k_ref, vt_ref, gv_ref, acc, dq, kt, rxc, ytx, rxy, rsum, ztx, zrx, ftx, frx, dqtx, dqrx, gtx, grx,
+    ds_ref, k_ref, vt_ref, acc, dq, kt, rxc, ytx, rxy, rsum, ztx, zrx, htx, frx, dqtx, dqrx, gtx, grx,
     bx_s, bx_r, ks_s, ks_r, zr_s, zr_r, sb_s, sb_r, pq_s, pq_r, ex_s, ex_r, kc_s, kc_r,
     ky_s, ky_r, zq_s, zq_r, f_s, f_r, g_s, g_r, o_s,
 ):
@@ -85,18 +85,32 @@
     ypart = dev(yl_=1 - yl)
     hpart = dev(yh_=1 - yh)
     cross = dev(yh_=1 - yh, yl_=1 - yl)
-    swap = dev(yh_=yl, yl_=yh)
     is_home = yh == yl
+    self_home = jnp.logical_and(is_home, jnp.logical_and(z // 4 == c, lax.rem(z, 2) == c))
 
     barrier = pltpu.get_barrier_semaphore()
-    for to in (xp, xm, zp, zm, sib, ypart, hpart, cross):
+    def greet(to):
         pl.semaphore_signal(barrier, inc=1, device_id=to, device_id_type=pl.DeviceIdType.MESH)
 
+    for to in (xp, xm, sib, ypart, hpart, cross):
+        greet(to)
+    for i in range(1, 8):
+        greet(dev(z_=zs[i]))
+    for i in range(4):
+        @pl.when(jnp.logical_not(jnp.logical_and(self_home, z // 2 == i)))
+        def _():
+            greet(dev(yh_=yl, yl_=yh, z_=2 * i + c, c_=z // 4))
+
+        @pl.when(jnp.logical_not(jnp.logical_and(self_home, lax.rem(z, 4) == i)))
+        def _():
+            greet(dev(yh_=yl, yl_=yh, z_=4 * c + i, c_=lax.rem(z, 2)))
+
+
     gain_row = gain[...]
     for r in range(ROWS):
         nb[r] = (normalised(codes, expo, r)[0] * gain_row).astype(BF)
 
-    pl.semaphore_wait(barrier, 8)
+    pl.semaphore_wait(barrier, jnp.where(self_home, 19, 21))
 
     bias_p = rc(bias, bias_g.at[0], bx_s.at[0], bx_r.at[0], xp)
     bias_m = rc(bias, bias_g.at[1], bx_s.at[1], bx_r.at[1], xm)
@@ -280,16 +294,13 @@
             gk[row] = nn(w[:, 128:256], qbd[...]).astype(BF)
 
         n = kn[row, pl.ds(pl.multiple_of(xb * KB, KB), KB), :]
-        for i in range(4):
-            rows = slice(i * 128, (i + 1) * 128)
-            kv = nn(n[rows, :], w[:, 128:384]).astype(BF)
-            k_ref[rows, :] = kv[:, 0:128]
-            vals[slot, rows, :] = kv[:, 128:256]
-        for i in range(2):
-            lanes = slice(i * 256, (i + 1) * 256)
-            keys_t[slot, :, lanes] = nt(wt[128:256, :], n[lanes, :]).astype(BF)
-            vt_ref[0:64, lanes] = nt(wt[256:320, :], n[lanes, :]).astype(BF)
-            vt_ref[80:144, lanes] = nt(wt[320:384, :], n[lanes, :]).astype(BF)
+        kv = nn(n, w[:, 128:384]).astype(BF)
+        kvt = nt(wt[128:384, :], n).astype(BF)
+        k_ref[...] = kv[:, 0:128]
+        vals[slot] = kv[:, 128:256]
+        keys_t[slot] = kvt[0:128, :]
+        vt_ref[0:64, :] = kvt[128:192, :]
+        vt_ref[80:144, :] = kvt[192:256, :]
         for hp in range(2):
             cols = slice(hp * 256, hp * 256 + 256)
             q2 = qbd[:, cols]
@@ -356,33 +367,64 @@
     rc(set_of(dot, yh), set_of(dot, 1 - yh), pq_s.at[1], pq_r.at[1], hpart).wait_recv()
     dq[...] = jnp.zeros_like(dq)
 
-    order = [xs[2], xs[1], xs[3], xs[0]]
-
-    def core_copy(zz):
-        return rc(kt.at[:, key_at(zz, 1 - c)], rxc.at[zz], kc_s.at[zz], kc_r.at[zz], sib)
-
-    def y_copy(zz):
-        return rc(ytx.at[zz], rxy.at[zz], ky_s.at[zz], ky_r.at[zz], ypart)
-
-    def core_stage(xb):
-        for b in range(2):
-            core_copy(xb * 2 + b).start()
+    def core_half(xb, cc):
+        return pl.ds(pl.multiple_of(xb * KB + cc * 256, 256), 256)
+
+    def z_part(zz):
+        return pl.ds(pl.multiple_of(zz * 32, 32), 32)
+
+    def core_copy(xb):
+        return rc(kt.at[:, core_half(xb, 1 - c)], rxc.at[xb], kc_s.at[xb], kc_r.at[xb], sib)
+
+    def y_copy(xb):
+        return rc(ytx.at[xb], rxy.at[xb], ky_s.at[xb], ky_r.at[xb], ypart)
+
+    def z_copy(xb, i):
+        return rc(
+            ztx.at[xb, :, z_part(zs[i])], zrx.at[xb, i], zq_s.at[xb, i], zq_r.at[xb, i], dev(z_=zs[i])
+        )
+
+    def own_copy(xb):
+        part = lax.rem(z, 4)
+        return rc(
+            htx.at[xb], frx.at[:, z_part(part)], f_s.at[xb], f_r.at[part],
+            dev(yh_=yl, yl_=yh, z_=2 * xb + c, c_=z // 4),
+        )
 
     def y_stage(xb):
-        for b in range(2):
-            zz = xb * 2 + b
-            core_copy(zz).wait_recv()
-            for r in range(ROWS):
-                theirs, ours = (1 - yl) * ROWS + r, yl * ROWS + r
-                ytx[zz, r] = (kt[theirs, key_at(zz, c), :].astype(F32) + rxc[zz, theirs].astype(F32)).astype(BF)
-                rsum[zz, r] = kt[ours, key_at(zz, c), :].astype(F32) + rxc[zz, ours].astype(F32)
-            y_copy(zz).start()
-
-    def sum_stage(xb):
-        for b in range(2):
-            zz = xb * 2 + b
-            y_copy(zz).wait_recv()
-            rsum[zz] = rsum[zz] + rxy[zz].astype(F32)
+        core_copy(xb).wait_recv()
+        for r in range(ROWS):
+            theirs, ours = (1 - yl) * ROWS + r, yl * ROWS + r
+            ytx[xb, r] = (kt[theirs, core_half(xb, c), :].astype(F32) + rxc[xb, theirs].astype(F32)).astype(BF)
+        y_copy(xb).start()
+        for r in range(ROWS):
+            ours = yl * ROWS + r
+            rsum[xb, r] = kt[ours, core_half(xb, c), :].astype(F32) + rxc[xb, ours].astype(F32)
+
+    def z_stage(xb):
+        y_copy(xb).wait_recv()
+        for r in range(ROWS):
+            total = rsum[xb, r] + rxy[xb, r].astype(F32)
+            rsum[xb, r] = total
+            ztx[xb, r] = total.astype(BF)
+        for i in (4, 3, 5, 2, 6, 1, 7):
+            z_copy(xb, i).start()
+
+    def home_stage(xb):
+        total = rsum[xb, :, z_part(z), :]
+        for i in range(1, 8):
+            z_copy(xb, i).wait_recv()
+            total = total + zrx[xb, i].astype(F32)
+        htx[xb] = total.astype(BF)
+        stays = jnp.logical_and(self_home, z // 2 == xb)
+
+        @pl.when(stays)
+        def _():
+            frx[:, z_part(lax.rem(z, 4)), :] = htx[xb]
+
+        @pl.when(jnp.logical_not(stays))
+        def _():
+            own_copy(xb).start()
 
     g_half_p = rc(gtx.at[0, pl.ds(0, 2)], grx.at[0, pl.ds(0, 2)], g_s.at[0], g_r.at[0], xp)
     g_half_m = rc(gtx.at[0, pl.ds(2, 2)], grx.at[0, pl.ds(2, 2)], g_s.at[1], g_r.at[1], xm)
@@ -441,6 +483,7 @@
         for h in range(HEADS):
             rows = slice(h * 32, (h + 1) * 32)
             dos[rows, h * 128 : (h + 1) * 128] = (dot[row, rows, :].astype(F32) * f[h : h + 1, :]).astype(BF)
+        keys = pl.ds(pl.multiple_of(xb * KB, KB), KB)
         key_t = keys_t[slot]
         for hp in range(2):
             cols = slice(hp * 256, hp * 256 + 256)
@@ -455,23 +498,32 @@
             for j in range(2):
                 rows = slice((hp * 2 + j) * 32, (hp * 2 + j + 1) * 32)
                 dq[row, rows, :] = dq[row, rows, :] + d_query[j * 32 : (j + 1) * 32, j * 128 : (j + 1) * 128]
-        for i in range(2):
-            lanes = slice(i * 256, (i + 1) * 256)
-            gv_ref[:, lanes] = nn(w[:, 256:384], dos[:, lanes]).astype(BF)
-        for i in range(4):
-            rows = slice(i * 128, (i + 1) * 128)
-            term = nt(ds_ref[rows, :], gk[row]) + nt(probs[slot, rows, :], gv_ref[...])
-            kt[row, pl.ds(pl.multiple_of(xb * KB + i * 128, 128), 128), :] = term.astype(BF)
-
-        for s in range(4):
+        gv = nn(w[:, 256:384], dos[...]).astype(BF)
+        kt[row, keys, :] = (nt(ds_ref[...], gk[row]) + nt(probs[slot], gv)).astype(BF)
+
+        def block_at(back):
+            return lax.rem(x + jnp.where(step == back, 2, jnp.where(step == back + 1, 1, 3)), NX)
+
+        @pl.when(jnp.logical_and(step >= 1, lax.rem(u, 6) == 1))
+        def _():
+            y_stage(block_at(1))
+
+        @pl.when(jnp.logical_and(step >= 2, lax.rem(u, 6) == 3))
+        def _():
+            home_stage(block_at(2))
+
+        @pl.when(jnp.logical_and(step >= 1, lax.rem(u, 6) == 5))
+        def _():
+            z_stage(block_at(1))
+
+        @pl.when(lax.rem(u, 6) == 5)
+        def _():
+            core_copy(xb).start()
+
+        for s in range(3):
             @pl.when(u == 6 * s + 5)
             def _():
-                bias_stage(s) if s < 3 else None
-                core_stage(order[s])
-                if s >= 1:
-                    y_stage(order[s - 1])
-                if s >= 2:
-                    sum_stage(order[s - 2])
+                bias_stage(s)
 
         return carry
 
@@ -479,64 +531,24 @@
 
     for r in range(ROWS):
         dqtx[r] = dq[(1 - yh) * ROWS + r].astype(BF)
-    dq_copy = rc(dqtx, dqrx, f_s.at[0], f_r.at[0], hpart)
+    dq_copy = rc(dqtx, dqrx, f_s.at[4], f_r.at[4], hpart)
     dq_copy.start()
-    y_stage(order[3])
-    sum_stage(order[2])
-    sum_stage(order[3])
-
-    def z_copy(way, i):
-        if i == 0:
-            part = pl.ds(way * 64, 64)
-            src, dst = ztx.at[way, 0, :, part], zrx.at[way, 0, :, part]
-        else:
-            src, dst = ztx.at[way, i], zrx.at[way, i]
-        return rc(src, dst, zq_s.at[way, i], zq_r.at[way, i], zp if way == 0 else zm)
-
-    for i in range(4):
-        for way in range(2):
-            home = zs[(4 - i) if way == 0 else (4 + i)]
-            if i == 0:
-                part = slice(way * 64, way * 64 + 64)
-                ztx[way, 0, :, part, :] = rsum[home, :, part, :].astype(BF)
-            else:
-                z_copy(way, i - 1).wait_recv()
-                if i == 1:
-                    part = slice(way * 64, way * 64 + 64)
-                    other = slice(64 - way * 64, 128 - way * 64)
-                    ztx[way, 1, :, part, :] = (
-                        rsum[home, :, part, :] + zrx[way, 0, :, part, :].astype(F32)
-                    ).astype(BF)
-                    ztx[way, 1, :, other, :] = rsum[home, :, other, :].astype(BF)
-                else:
-                    ztx[way, i] = (rsum[home] + zrx[way, i - 1].astype(F32)).astype(BF)
-            z_copy(way, i).start()
+    y_stage(x)
     bias_stage(3)
     bias_out = pltpu.make_async_copy(bias_grad, bias_hbm, o_s.at[1])
     bias_out.start()
-    z_copy(0, 3).wait_recv()
-    z_copy(1, 3).wait_recv()
-    ftx[...] = (rsum[z] + zrx[0, 3].astype(F32) + zrx[1, 3].astype(F32)).astype(BF)
-    final = rc(ftx, frx, f_s.at[1], f_r.at[1], swap)
-
-    @pl.when(jnp.logical_not(is_home))
-    def _():
-        final.start()
-
-    @pl.when(is_home)
-    def _():
-        frx[...] = ftx[...]
-
     dq_copy.wait_recv()
     for r in range(ROWS):
         d_query = (dq[yh * ROWS + r] + dqrx[r].astype(F32)) * (DH ** -0.5)
         unit_t = split_nn(w[:, 0:128], d_query) + split_nn(w[:, 384:512], dgp[r])
         dgated[r] = unit_t.T
-
-    @pl.when(jnp.logical_not(is_home))
-    def _():
-        final.wait_recv()
-
+    z_stage(x)
+    home_stage(xs[3])
+    home_stage(x)
+    for j in range(4):
+        @pl.when(jnp.logical_not(jnp.logical_and(self_home, lax.rem(z, 4) == j)))
+        def _():
+            rc(htx.at[0], frx.at[:, pl.ds(j * 32, 32)], f_s.at[0], f_r.at[j], sib).wait_recv()
     for r in range(ROWS):
         dgated[r] = dgated[r] + frx[r].astype(F32)
     normed_out = pltpu.make_async_copy(dgated, normed_hbm, o_s.at[2])
@@ -552,16 +564,17 @@
     for i in range(4):
         up(i).wait_send()
         down(i).wait_send()
-        z_copy(0, i).wait_send()
-        z_copy(1, i).wait_send()
+        core_copy(i).wait_send()
+        y_copy(i).wait_send()
+        for j in range(1, 8):
+            z_copy(i, j).wait_send()
+
+        @pl.when(jnp.logical_not(jnp.logical_and(self_home, z // 2 == i)))
+        def _():
+            own_copy(i).wait_send()
+
     for i in range(8):
         to_sib(i).wait_send()
-        core_copy(zs[i]).wait_send()
-        y_copy(zs[i]).wait_send()
-
-    @pl.when(jnp.logical_not(is_home))
-    def _():
-        final.wait_send()
 
     update_out.wait()
     bias_out.wait()
@@ -581,13 +594,13 @@
         vm((24, KB, C), BF), vm((24, C, KB), BF), vm((6, C, 512), BF), vm((6, C, T), F32), vm((6, 8, T), F32),
         vm(blk, BF), vm(blk, BF), vm((ROWS, 8, T), F32), vm((ROWS, 8, T), F32), vm((ROWS, 8, T), F32),
         vm((6, 8, T), F32), vm(blk, F32),
-        vm((KB, 512), BF), vm((KB, C), BF), vm((160, KB), BF), vm((C, 512), BF), vm((KB, 512), F32), vm((6, C, T), F32), vm((6, 2048, C), BF),
-        vm((8, 6, T, C), BF), vm((8, 3, T, C), BF), vm((8, 3, T, C), BF), vm((8, 3, T, C), F32),
-        vm((2, 4, 3, T, C), BF), vm((2, 4, 3, T, C), BF), vm(blk, BF), vm(blk, BF), vm(blk, BF), vm(blk, BF),
+        vm((KB, 512), BF), vm((KB, C), BF), vm((160, KB), BF), vm((KB, 512), F32), vm((6, C, T), F32), vm((6, 2048, C), BF),
+        vm((4, 6, 256, C), BF), vm((4, 3, 256, C), BF), vm((4, 3, 256, C), BF), vm((4, 3, 256, C), F32),
+        vm((4, 3, 256, C), BF), vm((4, 8, 3, 32, C), BF), vm((4, 3, 32, C), BF), vm(blk, BF), vm(blk, BF), vm(blk, BF),
         vm((3, HEADS, T, KB), BF), vm((3, HEADS, T, KB), BF),
         dma((4,)), dma((4,)), dma((2,)), dma((2,)), dma((2, 4)), dma((2, 4)), dma((8,)), dma((8,)),
-        dma((2,)), dma((2,)), dma((3,)), dma((3,)), dma((8,)), dma((8,)), dma((8,)), dma((8,)),
-        dma((2, 4)), dma((2, 4)), dma((2,)), dma((2,)), dma((4,)), dma((4,)), dma((3,)),
+        dma((2,)), dma((2,)), dma((3,)), dma((3,)), dma((4,)), dma((4,)), dma((4,)), dma((4,)),
+        dma((4, 8)), dma((4, 8)), dma((5,)), dma((5,)), dma((4,)), dma((4,)), dma((3,)),
     ]
     v = pl.BlockSpec(memory_space=pltpu.VMEM)
     hbm = pl.BlockSpec(memory_space=pl.ANY)

time: 120 us -> 117 us (0.975)
  the two profiles are of different devices: /device:TPU:8 before, /device:TPU:1 now
where the time goes in v3:
time: 117 us
  Pallas kernels  116 us (99%)
  between operations  1.28 us (1%)
    pallas_call x1, Pallas kernels, shards(): pl.pallas_call(kernel, out_shape=shapes, in_specs=[v] * 8, out_specs=(hbm...  113 us
    pallas_call x1, Pallas kernels, shards(): pl.pallas_call(norm_back, out_shape=(shapes[0], shapes[0], shapes[2]), in...  2.53 us

profile of v3, /device:TPU:1, one launch (start us, length us, event | category | flops | bytes accessed | tf_op | source)
XLA Modules:
  0.0 117.1 jit_solution(9697817022177564031)
XLA Ops:
  1.3 113.3 %shard_map.103 = (bf16[3,128,128]{2,1,0:T(8,128)(2,1)}, f32[3,128,128]{2,1,0:T(8,128)}, bf16[4,128,512]{2,1,0:T(8,128)(2,1)}) custom-call(s32[1]{0:T(128)S(6)} %copy.11.tok, bf16[3,128,128]{2,1,0:T(8,128)(2,1)} %codes.3, s32[1,3]{1,0:T(1,128)} %bitcast.2, f32[1,128]{1,0:T(1,128)} %bitcast.4, bf16[128,512]{1,0:T(8,128)(2,1)} %w.1, bf16[128,128]{1,0:T(8,128)(2,1)} %wo.1, ...), custom_call_target="tpu_custom_call" | custom-call | flops 8000000000 | bytes 4000000 | tf_op jit(solution)/shard_map/pallas_call | solution.py:613
  114.6 2.5 %shard_map.104 = (bf16[3,128,128]{2,1,0:T(8,128)(2,1)}, bf16[3,128,128]{2,1,0:T(8,128)(2,1)}, bf16[4,128,512]{2,1,0:T(8,128)(2,1)}) custom-call(bf16[3,128,128]{2,1,0:T(8,128)(2,1)} %codes.3, s32[1,3]{1,0:T(1,128)} %bitcast.3, f32[1,128]{1,0:T(1,128)} %bitcast.5, f32[3,128,128]{2,1,0:T(8,128)} %get-tuple-element.6.d_normed, ...), custom_call_target="tpu_custom_call" | custom-call | tf_op jit(solution)/shard_map/pallas_call | solution.py:624

commit v4 on v3

--- a/solution.py
+++ b/solution.py
@@ -60,7 +60,7 @@
     update, bias_grad,
     wt, wot, nb, gates, dgated, kn, qt, dot, bias_g, bias_t, probs, s_ref, qbd, dos,
     m_st, l_st, a_st, vals, keys_t, gk, att_loc, st_loc, att_tx, att_rx, st_rx, back_tx, back_rx, stats, dgp,
-    ds_ref, k_ref, vt_ref, acc, dq, kt, rxc, ytx, rxy, rsum, ztx, zrx, htx, frx, dqtx, dqrx, gtx, grx,
+    ds_ref, k_ref, vt_ref, gv_ref, acc, dq, kt, rxc, ytx, rxy, rsum, ztx, zrx, htx, frx, dqtx, dqrx, gtx, grx,
     bx_s, bx_r, ks_s, ks_r, zr_s, zr_r, sb_s, sb_r, pq_s, pq_r, ex_s, ex_r, kc_s, kc_r,
     ky_s, ky_r, zq_s, zq_r, f_s, f_r, g_s, g_r, o_s,
 ):
@@ -234,108 +234,131 @@
         for i in ((0, 1, 7), (2, 6), (3, 5), (4,))[phase]:
             from_sib(i).wait_recv()
 
-    vt_ref[64:80, :] = jnp.ones((16, KB), BF)
-    vt_ref[144:160, :] = jnp.ones((16, KB), BF)
-
-    def load_q(row):
+    for r in range(ROWS):
+        vt_ref[r, 64:80, :] = jnp.ones((16, KB), BF)
+        vt_ref[r, 144:160, :] = jnp.ones((16, KB), BF)
+
+    def load_q(r, row):
         for h in range(HEADS):
-            qbd[h * 32 : (h + 1) * 32, h * 128 : (h + 1) * 128] = qt[row, h * 32 : (h + 1) * 32, :]
+            qbd[r, h * 32 : (h + 1) * 32, h * 128 : (h + 1) * 128] = qt[row, h * 32 : (h + 1) * 32, :]
 
     att_copy = rc(att_tx, att_rx, ex_s.at[0], ex_r.at[0], hpart)
     st_copy = rc(set_of(st_loc, 1 - yh), st_rx, ex_s.at[1], ex_r.at[1], hpart)
     back_copy = rc(back_tx, back_rx, ex_s.at[2], ex_r.at[2], hpart)
 
-    def combine(row):
-        m_all = [m_st[row * 4 + i] for i in range(4)]
+    def combine(side, r):
+        m_all = [m_st[side * 4 + i, r] for i in range(4)]
         top_m = jnp.maximum(jnp.maximum(m_all[0], m_all[1]), jnp.maximum(m_all[2], m_all[3]))
         total = jnp.zeros((HEADS, T), F32)
         weighted = jnp.zeros((C, T), F32)
         for i in range(4):
             f = jnp.exp(m_all[i] - top_m)
-            total = total + f * l_st[row * 4 + i]
-            weighted = weighted + per_head(f) * a_st[row * 4 + i]
-        st_loc[row, 0:4, :] = top_m
-        st_loc[row, 4:8, :] = total
+            total = total + f * l_st[side * 4 + i, r]
+            weighted = weighted + per_head(f) * a_st[side * 4 + i, r]
+        st_loc[side * ROWS + r, 0:4, :] = top_m
+        st_loc[side * ROWS + r, 4:8, :] = total
         return weighted
 
     def forward(u, carry):
-        phase, t = u // 6, lax.rem(u, 6)
-        row = lax.rem(jnp.where(phase == 3, 1 - yh, yh) * ROWS + t, 2 * ROWS)
+        phase, second = u // 2, lax.rem(u, 2)
+        side = lax.rem(jnp.where(phase == 3, 1 - yh, yh) + second, 2)
         xb = lax.rem(
             jnp.where(phase == 0, zb, jnp.where(phase == 1, near, jnp.where(phase == 2, far, zb + 2))), NX
         )
-        slot = row * 4 + xb
+        sx = side * 4 + xb
 
         for i in range(4):
-            @pl.when(u == 6 * i)
+            @pl.when(u == 2 * i)
             def _():
                 arrive(i)
 
-        @pl.when(jnp.logical_and(t == 0, xb == xs[2]))
+        @pl.when(jnp.logical_and(second == 0, xb == xs[2]))
         def _():
             bias_fp.wait_recv()
             bias_fm.wait_recv()
             prep(bias_g.at[2], xs[2])
 
         for i in range(1, 4):
-            @pl.when(u == 6 * i - 3)
+            @pl.when(u == 2 * i - 1)
             def _():
                 ring_step(i)
 
-        @pl.when(u == 3)
+        @pl.when(u == 1)
         def _():
             rc(set_of(qt, yh), set_of(qt, 1 - yh), pq_s.at[0], pq_r.at[0], hpart).wait_recv()
             d_send.start()
 
-        load_q(row)
-
-        @pl.when(u < 6)
-        def _():
-            gk[row] = nn(w[:, 128:256], qbd[...]).astype(BF)
-
-        n = kn[row, pl.ds(pl.multiple_of(xb * KB, KB), KB), :]
-        kv = nn(n, w[:, 128:384]).astype(BF)
-        kvt = nt(wt[128:384, :], n).astype(BF)
-        k_ref[...] = kv[:, 0:128]
-        vals[slot] = kv[:, 128:256]
-        keys_t[slot] = kvt[0:128, :]
-        vt_ref[0:64, :] = kvt[128:192, :]
-        vt_ref[80:144, :] = kvt[192:256, :]
-        for hp in range(2):
+        for r in range(ROWS):
+            row = side * ROWS + r
+            load_q(r, row)
+            n = kn[row, pl.ds(pl.multiple_of(xb * KB, KB), KB), :]
+            kv = nn(n, w[:, 128:384]).astype(BF)
+            kvt = nt(wt[128:384, :], n).astype(BF)
+            k_ref[r] = kv[:, 0:128]
+            vals[sx, r] = kv[:, 128:256]
+            keys_t[sx, r] = kvt[0:128, :]
+            vt_ref[r, 0:64, :] = kvt[128:192, :]
+            vt_ref[r, 80:144, :] = kvt[192:256, :]
+
+        items = [(r, hp) for r in range(ROWS) for hp in range(2)]
+        tops = {}
+
+        def score(t):
+            r, hp = items[t]
             cols = slice(hp * 256, hp * 256 + 256)
-            q2 = qbd[:, cols]
+            q2 = qbd[r, :, cols]
             top = None
             for i in range(4):
                 rows = slice(i * 128, (i + 1) * 128)
-                s = nn(k_ref[rows, :], q2) + bias_t[xb, rows, cols]
-                s_ref[rows, cols] = s
+                s = nn(k_ref[r, rows, :], q2) + bias_t[xb, rows, cols]
+                s_ref[t % 3, rows, :] = s
                 part = jnp.max(s.reshape(16, 8, 256), axis=0)
                 top = part if top is None else jnp.maximum(top, part)
-            m = jnp.max(top, axis=0, keepdims=True)
+            tops[t] = jnp.max(top, axis=0, keepdims=True)
+
+        def weigh(t):
+            r, hp = items[t]
+            cols = slice(hp * 256, hp * 256 + 256)
             for i in range(4):
                 rows = slice(i * 128, (i + 1) * 128)
-                probs[slot, rows, cols] = jnp.exp(s_ref[rows, cols] - m).astype(BF)
-            a = nn(vt_ref[hp * 80 : hp * 80 + 80, :], probs[slot, :, cols])
+                probs[sx, r, rows, cols] = jnp.exp(s_ref[t % 3, rows, :] - tops[t]).astype(BF)
+
+        def attend(t):
+            r, hp = items[t]
+            cols = slice(hp * 256, hp * 256 + 256)
+            a = nn(vt_ref[r, hp * 80 : hp * 80 + 80, :], probs[sx, r, :, cols])
             for j in range(2):
                 h = hp * 2 + j
                 lanes = slice(j * 128, (j + 1) * 128)
-                m_st[slot, h : h + 1, :] = m[:, lanes]
-                l_st[slot, h : h + 1, :] = a[64:65, lanes]
-                a_st[slot, h * 32 : (h + 1) * 32, :] = a[j * 32 : (j + 1) * 32, lanes]
-
-        @pl.when(u == 20)
+                m_st[sx, r, h : h + 1, :] = tops[t][:, lanes]
+                l_st[sx, r, h : h + 1, :] = a[64:65, lanes]
+                a_st[sx, r, h * 32 : (h + 1) * 32, :] = a[j * 32 : (j + 1) * 32, lanes]
+
+        for t in range(8):
+            if t < 6:
+                score(t)
+            if 1 <= t < 7:
+                weigh(t - 1)
+            if t >= 2:
+                attend(t - 2)
+
+        @pl.when(u == 6)
         def _():
             for r in range(ROWS):
-                att_tx[r] = combine((1 - yh) * ROWS + r).astype(BF)
+                att_tx[r] = combine(1 - yh, r).astype(BF)
             att_copy.start()
             st_copy.start()
 
         return carry
 
-    lax.fori_loop(0, 24, forward, 0)
-
-    for r in range(ROWS):
-        att_loc[yh * ROWS + r] = combine(yh * ROWS + r)
+    lax.fori_loop(0, 8, forward, 0)
+
+    for row in range(6):
+        load_q(0, row)
+        gk[row] = nn(w[:, 128:256], qbd[0]).astype(BF)
+
+    for r in range(ROWS):
+        att_loc[yh * ROWS + r] = combine(yh, r)
     att_copy.wait_recv()
     st_copy.wait_recv()
     for r in range(ROWS):
@@ -462,87 +485,100 @@
             g_m.start()
 
     def backward(u, carry):
-        step = u // 6
+        step, second = u // 2, lax.rem(u, 2)
+        side = lax.rem(yh + second, 2)
         xb = lax.rem(x + jnp.where(step == 0, 2, jnp.where(step == 1, 1, jnp.where(step == 2, 3, 0))), NX)
-        row = lax.rem(yh * ROWS + lax.rem(u, 6), 2 * ROWS)
-        slot = row * 4 + xb
-
-        @pl.when(u == 3)
+        sx = side * 4 + xb
+
+        @pl.when(u == 1)
         def _():
             back_copy.wait_recv()
             for r in range(ROWS):
                 stats[(1 - yh) * ROWS + r] = back_rx[r]
 
-        @pl.when(lax.rem(u, 6) == 0)
+        @pl.when(second == 0)
         def _():
             acc[...] = jnp.zeros_like(acc)
 
-        st = stats[row]
-        f = jnp.exp(m_st[slot] - st[0:4, :])
-        dls = f * st[4:8, :]
-        for h in range(HEADS):
-            rows = slice(h * 32, (h + 1) * 32)
-            dos[rows, h * 128 : (h + 1) * 128] = (dot[row, rows, :].astype(F32) * f[h : h + 1, :]).astype(BF)
-        keys = pl.ds(pl.multiple_of(xb * KB, KB), KB)
-        key_t = keys_t[slot]
+        deltas, gvs = [], []
+        for r in range(ROWS):
+            row = side * ROWS + r
+            st = stats[row]
+            f = jnp.exp(m_st[sx, r] - st[0:4, :])
+            dls = f * st[4:8, :]
+            deltas.append([jnp.concatenate([dls[h : h + 1, :], dls[h + 1 : h + 2, :]], axis=1) for h in (0, 2)])
+            for h in range(HEADS):
+                rows = slice(h * 32, (h + 1) * 32)
+                dos[r, rows, h * 128 : (h + 1) * 128] = (
+                    dot[row, rows, :].astype(F32) * f[h : h + 1, :]
+                ).astype(BF)
+        for r in range(ROWS):
+            gv_ref[r] = nn(w[:, 256:384], dos[r]).astype(BF)
         for hp in range(2):
             cols = slice(hp * 256, hp * 256 + 256)
-            d2 = dos[:, cols]
-            l2 = jnp.concatenate([dls[hp * 2 : hp * 2 + 1, :], dls[hp * 2 + 1 : hp * 2 + 2, :]], axis=1)
             for i in range(4):
                 rows = slice(i * 128, (i + 1) * 128)
-                d_score = probs[slot, rows, cols].astype(F32) * (nn(vals[slot, rows, :], d2) - l2)
-                acc[rows, cols] = acc[rows, cols] + d_score
-                ds_ref[rows, cols] = d_score.astype(BF)
-            d_query = nn(key_t[hp * 64 : hp * 64 + 64, :], ds_ref[:, cols])
-            for j in range(2):
-                rows = slice((hp * 2 + j) * 32, (hp * 2 + j + 1) * 32)
-                dq[row, rows, :] = dq[row, rows, :] + d_query[j * 32 : (j + 1) * 32, j * 128 : (j + 1) * 128]
-        gv = nn(w[:, 256:384], dos[...]).astype(BF)
-        kt[row, keys, :] = (nt(ds_ref[...], gk[row]) + nt(probs[slot], gv)).astype(BF)
+                total = acc[rows, cols]
+                for r in range(ROWS):
+                    d_prob = nn(vals[sx, r, rows, :], dos[r, :, cols]) - deltas[r][hp]
+                    d_score = probs[sx, r, rows, cols].astype(F32) * d_prob
+                    total = total + d_score
+                    ds_ref[r, rows, cols] = d_score.astype(BF)
+                acc[rows, cols] = total
+            for r in range(ROWS):
+                row = side * ROWS + r
+                d_query = nn(keys_t[sx, r, hp * 64 : hp * 64 + 64, :], ds_ref[r, :, cols])
+                for j in range(2):
+                    rows = slice((hp * 2 + j) * 32, (hp * 2 + j + 1) * 32)
+                    dq[row, rows, :] = dq[row, rows, :] + d_query[j * 32 : (j + 1) * 32, j * 128 : (j + 1) * 128]
+        for r in range(ROWS):
+            row = side * ROWS + r
+            kt[row, pl.ds(pl.multiple_of(xb * KB, KB), KB), :] = (
+                nt(ds_ref[r], gk[row]) + nt(probs[sx, r], gv_ref[r])
+            ).astype(BF)
 
         def block_at(back):
             return lax.rem(x + jnp.where(step == back, 2, jnp.where(step == back + 1, 1, 3)), NX)
 
-        @pl.when(jnp.logical_and(step >= 1, lax.rem(u, 6) == 1))
+        @pl.when(jnp.logical_and(step >= 1, second == 0))
         def _():
             y_stage(block_at(1))
 
-        @pl.when(jnp.logical_and(step >= 2, lax.rem(u, 6) == 3))
+        @pl.when(jnp.logical_and(step >= 2, second == 0))
         def _():
             home_stage(block_at(2))
 
-        @pl.when(jnp.logical_and(step >= 1, lax.rem(u, 6) == 5))
+        @pl.when(second == 1)
+        def _():
+            core_copy(xb).start()
+
+        @pl.when(jnp.logical_and(step >= 1, second == 1))
         def _():
             z_stage(block_at(1))
 
-        @pl.when(lax.rem(u, 6) == 5)
-        def _():
-            core_copy(xb).start()
-
         for s in range(3):
-            @pl.when(u == 6 * s + 5)
+            @pl.when(u == 2 * s + 1)
             def _():
                 bias_stage(s)
 
         return carry
 
-    lax.fori_loop(0, 24, backward, 0)
+    lax.fori_loop(0, 8, backward, 0)
 
     for r in range(ROWS):
         dqtx[r] = dq[(1 - yh) * ROWS + r].astype(BF)
     dq_copy = rc(dqtx, dqrx, f_s.at[4], f_r.at[4], hpart)
     dq_copy.start()
     y_stage(x)
-    bias_stage(3)
-    bias_out = pltpu.make_async_copy(bias_grad, bias_hbm, o_s.at[1])
-    bias_out.start()
     dq_copy.wait_recv()
     for r in range(ROWS):
         d_query = (dq[yh * ROWS + r] + dqrx[r].astype(F32)) * (DH ** -0.5)
         unit_t = split_nn(w[:, 0:128], d_query) + split_nn(w[:, 384:512], dgp[r])
         dgated[r] = unit_t.T
     z_stage(x)
+    bias_stage(3)
+    bias_out = pltpu.make_async_copy(bias_grad, bias_hbm, o_s.at[1])
+    bias_out.start()
     home_stage(xs[3])
     home_stage(x)
     for j in range(4):
@@ -589,12 +625,14 @@
         vm(blk, BF), vm((HEADS, T, KB), BF),
         vm((512, C), BF), vm((C, C), BF), vm(blk, BF), vm(blk, F32), vm(blk, F32),
         vm((6, 2048, C), BF), vm((6, C, T), BF), vm((6, C, T), BF), vm((3, HEADS, T, KB), BF),
-        vm((4, KB, 512), F32), vm((24, KB, 512), BF), vm((KB, 512), F32), vm((C, 512), BF), vm((C, 512), BF),
-        vm((24, HEADS, T), F32), vm((24, HEADS, T), F32), vm((24, C, T), F32),
-        vm((24, KB, C), BF), vm((24, C, KB), BF), vm((6, C, 512), BF), vm((6, C, T), F32), vm((6, 8, T), F32),
+        vm((4, KB, 512), F32), vm((8, 3, KB, 512), BF), vm((3, KB, 256), F32), vm((3, C, 512), BF),
+        vm((3, C, 512), BF),
+        vm((8, 3, HEADS, T), F32), vm((8, 3, HEADS, T), F32), vm((8, 3, C, T), F32),
+        vm((8, 3, KB, C), BF), vm((8, 3, C, KB), BF), vm((6, C, 512), BF), vm((6, C, T), F32), vm((6, 8, T), F32),
         vm(blk, BF), vm(blk, BF), vm((ROWS, 8, T), F32), vm((ROWS, 8, T), F32), vm((ROWS, 8, T), F32),
         vm((6, 8, T), F32), vm(blk, F32),
-        vm((KB, 512), BF), vm((KB, C), BF), vm((160, KB), BF), vm((KB, 512), F32), vm((6, C, T), F32), vm((6, 2048, C), BF),
+        vm((3, KB, 512), BF), vm((3, KB, C), BF), vm((3, 160, KB), BF), vm((3, C, 512), BF), vm((KB, 512), F32),
+        vm((6, C, T), F32), vm((6, 2048, C), BF),
         vm((4, 6, 256, C), BF), vm((4, 3, 256, C), BF), vm((4, 3, 256, C), BF), vm((4, 3, 256, C), F32),
         vm((4, 3, 256, C), BF), vm((4, 8, 3, 32, C), BF), vm((4, 3, 32, C), BF), vm(blk, BF), vm(blk, BF), vm(blk, BF),
         vm((3, HEADS, T, KB), BF), vm((3, HEADS, T, KB), BF),

time: 117 us -> 106 us (0.906)
  Pallas kernels: 116 us -> 104 us
    pallas_call x1, Pallas kernels: 113 us -> 102 us  [shards(): pl.pallas_call(kernel, out_shape=shapes, in_specs=[v] * 8, out_specs=(hbm...]
where the time goes in v4:
time: 106 us
  Pallas kernels  104 us (98%)
  between operations  1.28 us (1%)
    pallas_call x1, Pallas kernels, shards(): pl.pallas_call(kernel, out_shape=shapes, in_specs=[v] * 8, out_specs=(hbm...  102 us
    pallas_call x1, Pallas kernels, shards(): pl.pallas_call(norm_back, out_shape=(shapes[0], shapes[0], shapes[2]), in...  2.53 us

profile of v4, /device:TPU:1, one launch (start us, length us, event | category | flops | bytes accessed | tf_op | source)
XLA Modules:
  0.0 105.7 jit_solution(8389379106757285320)
XLA Ops:
  1.3 101.9 %shard_map.103 = (bf16[3,128,128]{2,1,0:T(8,128)(2,1)}, f32[3,128,128]{2,1,0:T(8,128)}, bf16[4,128,512]{2,1,0:T(8,128)(2,1)}) custom-call(s32[1]{0:T(128)S(6)} %copy.11.tok, bf16[3,128,128]{2,1,0:T(8,128)(2,1)} %codes.3, s32[1,3]{1,0:T(1,128)} %bitcast.2, f32[1,128]{1,0:T(1,128)} %bitcast.4, bf16[128,512]{1,0:T(8,128)(2,1)} %w.1, bf16[128,128]{1,0:T(8,128)(2,1)} %wo.1, ...), custom_call_target="tpu_custom_call" | custom-call | flops 8000000000 | bytes 4000000 | tf_op jit(solution)/shard_map/pallas_call | solution.py:651
  103.2 2.5 %shard_map.104 = (bf16[3,128,128]{2,1,0:T(8,128)(2,1)}, bf16[3,128,128]{2,1,0:T(8,128)(2,1)}, bf16[4,128,512]{2,1,0:T(8,128)(2,1)}) custom-call(bf16[3,128,128]{2,1,0:T(8,128)(2,1)} %codes.3, s32[1,3]{1,0:T(1,128)} %bitcast.3, f32[1,128]{1,0:T(1,128)} %bitcast.5, f32[3,128,128]{2,1,0:T(8,128)} %get-tuple-element.6.d_normed, ...), custom_call_target="tpu_custom_call" | custom-call | tf_op jit(solution)/shard_map/pallas_call | solution.py:662

commit v5 on v4

--- a/solution.py
+++ b/solution.py
@@ -60,7 +60,7 @@
     update, bias_grad,
     wt, wot, nb, gates, dgated, kn, qt, dot, bias_g, bias_t, probs, s_ref, qbd, dos,
     m_st, l_st, a_st, vals, keys_t, gk, att_loc, st_loc, att_tx, att_rx, st_rx, back_tx, back_rx, stats, dgp,
-    ds_ref, k_ref, vt_ref, gv_ref, acc, dq, kt, rxc, ytx, rxy, rsum, ztx, zrx, htx, frx, dqtx, dqrx, gtx, grx,
+    ds_ref, k_ref, vt_ref, gv_ref, turned, dq, kt, rxc, ytx, rxy, rsum, ztx, zrx, htx, frx, dqtx, dqrx, gtx, grx,
     bx_s, bx_r, ks_s, ks_r, zr_s, zr_r, sb_s, sb_r, pq_s, pq_r, ex_s, ex_r, kc_s, kc_r,
     ky_s, ky_r, zq_s, zq_r, f_s, f_r, g_s, g_r, o_s,
 ):
@@ -352,10 +352,6 @@
         return carry
 
     lax.fori_loop(0, 8, forward, 0)
-
-    for row in range(6):
-        load_q(0, row)
-        gk[row] = nn(w[:, 128:256], qbd[0]).astype(BF)
 
     for r in range(ROWS):
         att_loc[yh * ROWS + r] = combine(yh, r)
@@ -387,7 +383,14 @@
         update[r] = nn(wot[...], (gate * attended).astype(BF)).T.astype(BF)
     update_out = pltpu.make_async_copy(update, update_hbm, o_s.at[0])
     update_out.start()
+    for row in range(6):
+        load_q(0, row)
+        gk[row] = nn(w[:, 128:256], qbd[0]).astype(BF)
+
     rc(set_of(dot, yh), set_of(dot, 1 - yh), pq_s.at[1], pq_r.at[1], hpart).wait_recv()
+    back_copy.wait_recv()
+    for r in range(ROWS):
+        stats[(1 - yh) * ROWS + r] = back_rx[r]
     dq[...] = jnp.zeros_like(dq)
 
     def core_half(xb, cc):
@@ -453,9 +456,6 @@
     g_half_m = rc(gtx.at[0, pl.ds(2, 2)], grx.at[0, pl.ds(2, 2)], g_s.at[1], g_r.at[1], xm)
     g_p = rc(gtx.at[1], grx.at[1], g_s.at[2], g_r.at[2], xp)
     g_m = rc(gtx.at[2], grx.at[2], g_s.at[3], g_r.at[3], xm)
-
-    def turned(h, k):
-        return acc[k * 128 : (k + 1) * 128, h * 128 : (h + 1) * 128].T
 
     def bias_stage(step):
         if step == 1:
@@ -468,7 +468,7 @@
         for h in range(HEADS):
             for k in range(4):
                 lanes = slice(k * 128, (k + 1) * 128)
-                tile = turned(h, k)
+                tile = turned[h, :, lanes]
                 if (step == 1 and h < 2) or (step == 2 and h >= 2):
                     tile = tile + grx[0, h, :, lanes].astype(F32)
                 if step == 3:
@@ -484,95 +484,76 @@
         if step == 2:
             g_m.start()
 
-    def backward(u, carry):
-        step, second = u // 2, lax.rem(u, 2)
-        side = lax.rem(yh + second, 2)
+    def backward(step, carry):
         xb = lax.rem(x + jnp.where(step == 0, 2, jnp.where(step == 1, 1, jnp.where(step == 2, 3, 0))), NX)
-        sx = side * 4 + xb
-
-        @pl.when(u == 1)
-        def _():
-            back_copy.wait_recv()
-            for r in range(ROWS):
-                stats[(1 - yh) * ROWS + r] = back_rx[r]
-
-        @pl.when(second == 0)
-        def _():
-            acc[...] = jnp.zeros_like(acc)
-
-        deltas, gvs = [], []
-        for r in range(ROWS):
-            row = side * ROWS + r
+        places = []
+        for q in range(2 * ROWS):
+            side = yh if q < ROWS else 1 - yh
+            places.append((side * 4 + xb, q % ROWS, side * ROWS + q % ROWS))
+
+        deltas = []
+        for q, (sx, r, row) in enumerate(places):
             st = stats[row]
             f = jnp.exp(m_st[sx, r] - st[0:4, :])
             dls = f * st[4:8, :]
             deltas.append([jnp.concatenate([dls[h : h + 1, :], dls[h + 1 : h + 2, :]], axis=1) for h in (0, 2)])
             for h in range(HEADS):
                 rows = slice(h * 32, (h + 1) * 32)
-                dos[r, rows, h * 128 : (h + 1) * 128] = (
+                dos[q, rows, h * 128 : (h + 1) * 128] = (
                     dot[row, rows, :].astype(F32) * f[h : h + 1, :]
                 ).astype(BF)
-        for r in range(ROWS):
-            gv_ref[r] = nn(w[:, 256:384], dos[r]).astype(BF)
+            gv_ref[q] = nn(w[:, 256:384], dos[q]).astype(BF)
         for hp in range(2):
             cols = slice(hp * 256, hp * 256 + 256)
             for i in range(4):
                 rows = slice(i * 128, (i + 1) * 128)
-                total = acc[rows, cols]
-                for r in range(ROWS):
-                    d_prob = nn(vals[sx, r, rows, :], dos[r, :, cols]) - deltas[r][hp]
+                total = None
+                for q, (sx, r, row) in enumerate(places):
+                    d_prob = nn(vals[sx, r, rows, :], dos[q, :, cols]) - deltas[q][hp]
                     d_score = probs[sx, r, rows, cols].astype(F32) * d_prob
-                    total = total + d_score
-                    ds_ref[r, rows, cols] = d_score.astype(BF)
-                acc[rows, cols] = total
-            for r in range(ROWS):
-                row = side * ROWS + r
-                d_query = nn(keys_t[sx, r, hp * 64 : hp * 64 + 64, :], ds_ref[r, :, cols])
+                    total = d_score if total is None else total + d_score
+                    ds_ref[q, rows, cols] = d_score.astype(BF)
+                for j in range(2):
+                    turned[hp * 2 + j, :, rows] = total[:, j * 128 : (j + 1) * 128].T
+            for q, (sx, r, row) in enumerate(places):
+                d_query = nn(keys_t[sx, r, hp * 64 : hp * 64 + 64, :], ds_ref[q, :, cols])
                 for j in range(2):
                     rows = slice((hp * 2 + j) * 32, (hp * 2 + j + 1) * 32)
-                    dq[row, rows, :] = dq[row, rows, :] + d_query[j * 32 : (j + 1) * 32, j * 128 : (j + 1) * 128]
-        for r in range(ROWS):
-            row = side * ROWS + r
+                    dq[q, rows, :] = dq[q, rows, :] + d_query[j * 32 : (j + 1) * 32, j * 128 : (j + 1) * 128]
+        for q, (sx, r, row) in enumerate(places):
             kt[row, pl.ds(pl.multiple_of(xb * KB, KB), KB), :] = (
-                nt(ds_ref[r], gk[row]) + nt(probs[sx, r], gv_ref[r])
+                nt(ds_ref[q], gk[row]) + nt(probs[sx, r], gv_ref[q])
             ).astype(BF)
 
         def block_at(back):
             return lax.rem(x + jnp.where(step == back, 2, jnp.where(step == back + 1, 1, 3)), NX)
 
-        @pl.when(jnp.logical_and(step >= 1, second == 0))
-        def _():
-            y_stage(block_at(1))
-
-        @pl.when(jnp.logical_and(step >= 2, second == 0))
-        def _():
-            home_stage(block_at(2))
-
-        @pl.when(second == 1)
-        def _():
-            core_copy(xb).start()
-
-        @pl.when(jnp.logical_and(step >= 1, second == 1))
-        def _():
-            z_stage(block_at(1))
-
+        core_copy(xb).start()
         for s in range(3):
-            @pl.when(u == 2 * s + 1)
+            @pl.when(step == s)
             def _():
                 bias_stage(s)
 
+        @pl.when(step >= 1)
+        def _():
+            z_stage(block_at(1))
+
+        @pl.when(step >= 2)
+        def _():
+            home_stage(block_at(2))
+
+        y_stage(xb)
         return carry
 
-    lax.fori_loop(0, 8, backward, 0)
-
-    for r in range(ROWS):
-        dqtx[r] = dq[(1 - yh) * ROWS + r].astype(BF)
+    lax.fori_loop(0, 4, backward, 0)
+
+    for r in range(ROWS):
+        dqtx[r] = dq[ROWS + r].astype(BF)
     dq_copy = rc(dqtx, dqrx, f_s.at[4], f_r.at[4], hpart)
     dq_copy.start()
-    y_stage(x)
     dq_copy.wait_recv()
     for r in range(ROWS):
-        d_query = (dq[yh * ROWS + r] + dqrx[r].astype(F32)) * (DH ** -0.5)
+        d_query = (dq[r] + dqrx[r].astype(F32)) * (DH ** -0.5)
         unit_t = split_nn(w[:, 0:128], d_query) + split_nn(w[:, 384:512], dgp[r])
         dgated[r] = unit_t.T
     z_stage(x)
@@ -626,12 +607,12 @@
         vm((512, C), BF), vm((C, C), BF), vm(blk, BF), vm(blk, F32), vm(blk, F32),
         vm((6, 2048, C), BF), vm((6, C, T), BF), vm((6, C, T), BF), vm((3, HEADS, T, KB), BF),
         vm((4, KB, 512), F32), vm((8, 3, KB, 512), BF), vm((3, KB, 256), F32), vm((3, C, 512), BF),
-        vm((3, C, 512), BF),
+        vm((6, C, 512), BF),
         vm((8, 3, HEADS, T), F32), vm((8, 3, HEADS, T), F32), vm((8, 3, C, T), F32),
         vm((8, 3, KB, C), BF), vm((8, 3, C, KB), BF), vm((6, C, 512), BF), vm((6, C, T), F32), vm((6, 8, T), F32),
         vm(blk, BF), vm(blk, BF), vm((ROWS, 8, T), F32), vm((ROWS, 8, T), F32), vm((ROWS, 8, T), F32),
         vm((6, 8, T), F32), vm(blk, F32),
-        vm((3, KB, 512), BF), vm((3, KB, C), BF), vm((3, 160, KB), BF), vm((3, C, 512), BF), vm((KB, 512), F32),
+        vm((6, KB, 512), BF), vm((3, KB, C), BF), vm((3, 160, KB), BF), vm((6, C, 512), BF), vm((HEADS, T, KB), F32),
         vm((6, C, T), F32), vm((6, 2048, C), BF),
         vm((4, 6, 256, C), BF), vm((4, 3, 256, C), BF), vm((4, 3, 256, C), BF), vm((4, 3, 256, C), F32),
         vm((4, 3, 256, C), BF), vm((4, 8, 3, 32, C), BF), vm((4, 3, 32, C), BF), vm(blk, BF), vm(blk, BF), vm(blk, BF),

time: 106 us -> 105 us (level)
  no operation moved by 1% of the time
where the time goes in v5:
time: 105 us
  Pallas kernels  104 us (99%)
  between operations  1.28 us (1%)
    pallas_call x1, Pallas kernels, shards(): pl.pallas_call(kernel, out_shape=shapes, in_specs=[v] * 8, out_specs=(hbm...  101 us
    pallas_call x1, Pallas kernels, shards(): pl.pallas_call(norm_back, out_shape=(shapes[0], shapes[0], shapes[2]), in...  2.53 us

profile of v5, /device:TPU:1, one launch (start us, length us, event | category | flops | bytes accessed | tf_op | source)
XLA Modules:
  0.0 105.0 jit_solution(16223836055559759484)
XLA Ops:
  1.3 101.2 %shard_map.103 = (bf16[3,128,128]{2,1,0:T(8,128)(2,1)}, f32[3,128,128]{2,1,0:T(8,128)}, bf16[4,128,512]{2,1,0:T(8,128)(2,1)}) custom-call(s32[1]{0:T(128)S(6)} %copy.11.tok, bf16[3,128,128]{2,1,0:T(8,128)(2,1)} %codes.3, s32[1,3]{1,0:T(1,128)} %bitcast.2, f32[1,128]{1,0:T(1,128)} %bitcast.4, bf16[128,512]{1,0:T(8,128)(2,1)} %w.1, bf16[128,128]{1,0:T(8,128)(2,1)} %wo.1, ...), custom_call_target="tpu_custom_call" | custom-call | flops 8000000000 | bytes 4000000 | tf_op jit(solution)/shard_map/pallas_call | solution.py:632
  102.5 2.5 %shard_map.104 = (bf16[3,128,128]{2,1,0:T(8,128)(2,1)}, bf16[3,128,128]{2,1,0:T(8,128)(2,1)}, bf16[4,128,512]{2,1,0:T(8,128)(2,1)}) custom-call(bf16[3,128,128]{2,1,0:T(8,128)(2,1)} %codes.3, s32[1,3]{1,0:T(1,128)} %bitcast.3, f32[1,128]{1,0:T(1,128)} %bitcast.5, f32[3,128,128]{2,1,0:T(8,128)} %get-tuple-element.6.d_normed, ...), custom_call_target="tpu_custom_call" | custom-call | tf_op jit(solution)/shard_map/pallas_call | solution.py:643

commit v6 on v5

--- a/solution.py
+++ b/solution.py
@@ -60,7 +60,7 @@
     update, bias_grad,
     wt, wot, nb, gates, dgated, kn, qt, dot, bias_g, bias_t, probs, s_ref, qbd, dos,
     m_st, l_st, a_st, vals, keys_t, gk, att_loc, st_loc, att_tx, att_rx, st_rx, back_tx, back_rx, stats, dgp,
-    ds_ref, k_ref, vt_ref, gv_ref, turned, dq, kt, rxc, ytx, rxy, rsum, ztx, zrx, htx, frx, dqtx, dqrx, gtx, grx,
+    ds_ref, k_ref, vt_ref, gv_ref, acc, turned, dq, kt, rxc, ytx, rxy, rsum, ztx, zrx, htx, frx, dqtx, dqrx, gtx, grx,
     bx_s, bx_r, ks_s, ks_r, zr_s, zr_r, sb_s, sb_r, pq_s, pq_r, ex_s, ex_r, kc_s, kc_r,
     ky_s, ky_r, zq_s, zq_r, f_s, f_r, g_s, g_r, o_s,
 ):
@@ -169,24 +169,21 @@
     dos[...] = jnp.zeros_like(dos)
     prep(bias, x)
 
-    for s in range(2):
-        @pl.when(jnp.logical_not(jnp.logical_and(is_home, yh == s)))
-        def _():
-            rc(nb, kn.at[pl.ds(s * ROWS, ROWS), key_at(z, c)], ks_s.at[0], ks_r.at[s], sib).wait_recv()
-
     def block(zz, cc=c):
         return kn.at[:, key_at(zz, cc)]
 
     def half(zz, s):
         return kn.at[pl.ds(s * ROWS, ROWS), key_at(zz, c)]
 
-    def up(i):
-        src = block(zs[(8 - i) % 8]) if i < 3 else half(zs[5], 0)
-        return rc(src, src, zr_s.at[0, i], zr_r.at[0, i], zp)
-
-    def down(i):
-        src = block(zs[i]) if i < 3 else half(zs[3], 1)
-        return rc(src, src, zr_s.at[1, i], zr_r.at[1, i], zm)
+    sides = [yh, 1 - yh]
+
+    def up(i, p):
+        src = half(zs[(8 - i) % 8], sides[p])
+        return rc(src, src, zr_s.at[0, i, p], zr_r.at[0, i, p], zp)
+
+    def down(i, p):
+        src = half(zs[i], sides[p])
+        return rc(src, src, zr_s.at[1, i, p], zr_r.at[1, i, p], zm)
 
     def to_sib(i):
         return rc(block(zs[i]), block(zs[i]), sb_s.at[i], sb_r.at[i], sib)
@@ -194,28 +191,43 @@
     def from_sib(i):
         return rc(block(zs[i], 1 - c), block(zs[i], 1 - c), sb_s.at[i], sb_r.at[i], sib)
 
-    def up_in(i):
-        dst = block(zs[7 - i]) if i < 3 else half(zs[4], 0)
-        return rc(dst, dst, zr_s.at[0, i], zr_r.at[0, i], zp)
-
-    def down_in(i):
-        dst = block(zs[i + 1]) if i < 3 else half(zs[4], 1)
-        return rc(dst, dst, zr_s.at[1, i], zr_r.at[1, i], zm)
+    def up_in(i, p):
+        dst = half(zs[7 - i], sides[p])
+        return rc(dst, dst, zr_s.at[0, i, p], zr_r.at[0, i, p], zp)
+
+    def down_in(i, p):
+        dst = half(zs[i + 1], sides[p])
+        return rc(dst, dst, zr_s.at[1, i, p], zr_r.at[1, i, p], zm)
+
+    def goes_up(i, p):
+        return i < 3 or (i == 3 and p == 0)
+
+    def goes_down(i, p):
+        return i < 3 or (i == 3 and p == 1)
 
     def ring_step(i):
-        up_in(i).wait_recv()
+        for p in range(2):
+            if goes_up(i, p):
+                up_in(i, p).wait_recv()
+                if goes_up(i + 1, p):
+                    up(i + 1, p).start()
+            if goes_down(i, p):
+                down_in(i, p).wait_recv()
+                if goes_down(i + 1, p):
+                    down(i + 1, p).start()
         if i < 3:
-            up(i + 1).start()
             to_sib(7 - i).start()
-        down_in(i).wait_recv()
-        if i < 3:
-            down(i + 1).start()
             to_sib(i + 1).start()
         else:
             to_sib(4).start()
 
-    up(0).start()
-    down(0).start()
+    for p in range(2):
+        @pl.when(jnp.logical_not(jnp.logical_and(is_home, p == 0)))
+        def _():
+            rc(nb, half(z, sides[p]), ks_s.at[0], ks_r.at[sides[p]], sib).wait_recv()
+
+        up(0, p).start()
+        down(0, p).start()
     to_sib(0).start()
     bias_p.wait_recv()
     bias_fp.start()
@@ -399,8 +411,11 @@
     def z_part(zz):
         return pl.ds(pl.multiple_of(zz * 32, 32), 32)
 
-    def core_copy(xb):
-        return rc(kt.at[:, core_half(xb, 1 - c)], rxc.at[xb], kc_s.at[xb], kc_r.at[xb], sib)
+    def core_copy(xb, p):
+        rows = pl.ds((yl if p else 1 - yl) * ROWS, ROWS)
+        return rc(
+            kt.at[rows, core_half(xb, 1 - c)], rxc.at[xb, rows], kc_s.at[xb, p], kc_r.at[xb, p], sib
+        )
 
     def y_copy(xb):
         return rc(ytx.at[xb], rxy.at[xb], ky_s.at[xb], ky_r.at[xb], ypart)
@@ -418,19 +433,19 @@
         )
 
     def y_stage(xb):
-        core_copy(xb).wait_recv()
+        core_copy(xb, 0).wait_recv()
         for r in range(ROWS):
-            theirs, ours = (1 - yl) * ROWS + r, yl * ROWS + r
+            theirs = (1 - yl) * ROWS + r
             ytx[xb, r] = (kt[theirs, core_half(xb, c), :].astype(F32) + rxc[xb, theirs].astype(F32)).astype(BF)
         y_copy(xb).start()
+
+    def z_stage(xb):
+        core_copy(xb, 1).wait_recv()
+        y_copy(xb).wait_recv()
         for r in range(ROWS):
             ours = yl * ROWS + r
-            rsum[xb, r] = kt[ours, core_half(xb, c), :].astype(F32) + rxc[xb, ours].astype(F32)
-
-    def z_stage(xb):
-        y_copy(xb).wait_recv()
-        for r in range(ROWS):
-            total = rsum[xb, r] + rxy[xb, r].astype(F32)
+            total = kt[ours, core_half(xb, c), :].astype(F32) + rxc[xb, ours].astype(F32)
+            total = total + rxy[xb, r].astype(F32)
             rsum[xb, r] = total
             ztx[xb, r] = total.astype(BF)
         for i in (4, 3, 5, 2, 6, 1, 7):
@@ -488,11 +503,11 @@
         xb = lax.rem(x + jnp.where(step == 0, 2, jnp.where(step == 1, 1, jnp.where(step == 2, 3, 0))), NX)
         places = []
         for q in range(2 * ROWS):
-            side = yh if q < ROWS else 1 - yh
-            places.append((side * 4 + xb, q % ROWS, side * ROWS + q % ROWS))
+            side = 1 - yl if q < ROWS else yl
+            places.append((q, side * 4 + xb, q % ROWS, side * ROWS + q % ROWS))
 
         deltas = []
-        for q, (sx, r, row) in enumerate(places):
+        for q, sx, r, row in places:
             st = stats[row]
             f = jnp.exp(m_st[sx, r] - st[0:4, :])
             dls = f * st[4:8, :]
@@ -503,32 +518,50 @@
                     dot[row, rows, :].astype(F32) * f[h : h + 1, :]
                 ).astype(BF)
             gv_ref[q] = nn(w[:, 256:384], dos[q]).astype(BF)
-        for hp in range(2):
+
+        def score_grads(group, hp):
             cols = slice(hp * 256, hp * 256 + 256)
             for i in range(4):
                 rows = slice(i * 128, (i + 1) * 128)
-                total = None
-                for q, (sx, r, row) in enumerate(places):
+                total = acc[rows, cols] if group else None
+                for q, sx, r, row in places[group * ROWS : group * ROWS + ROWS]:
                     d_prob = nn(vals[sx, r, rows, :], dos[q, :, cols]) - deltas[q][hp]
                     d_score = probs[sx, r, rows, cols].astype(F32) * d_prob
                     total = d_score if total is None else total + d_score
                     ds_ref[q, rows, cols] = d_score.astype(BF)
-                for j in range(2):
-                    turned[hp * 2 + j, :, rows] = total[:, j * 128 : (j + 1) * 128].T
-            for q, (sx, r, row) in enumerate(places):
+                if group:
+                    for j in range(2):
+                        turned[hp * 2 + j, :, rows] = total[:, j * 128 : (j + 1) * 128].T
+                else:
+                    acc[rows, cols] = total
+
+        def query_grads(group, hp):
+            cols = slice(hp * 256, hp * 256 + 256)
+            for q, sx, r, row in places[group * ROWS : group * ROWS + ROWS]:
                 d_query = nn(keys_t[sx, r, hp * 64 : hp * 64 + 64, :], ds_ref[q, :, cols])
                 for j in range(2):
                     rows = slice((hp * 2 + j) * 32, (hp * 2 + j + 1) * 32)
                     dq[q, rows, :] = dq[q, rows, :] + d_query[j * 32 : (j + 1) * 32, j * 128 : (j + 1) * 128]
-        for q, (sx, r, row) in enumerate(places):
-            kt[row, pl.ds(pl.multiple_of(xb * KB, KB), KB), :] = (
-                nt(ds_ref[q], gk[row]) + nt(probs[sx, r], gv_ref[q])
-            ).astype(BF)
+
+        def key_terms(group):
+            for q, sx, r, row in places[group * ROWS : group * ROWS + ROWS]:
+                kt[row, pl.ds(pl.multiple_of(xb * KB, KB), KB), :] = (
+                    nt(ds_ref[q], gk[row]) + nt(probs[sx, r], gv_ref[q])
+                ).astype(BF)
+
+        for group in range(2):
+            score_grads(group, 0)
+            query_grads(group, 0)
+            if group:
+                y_stage(xb)
+            score_grads(group, 1)
+            query_grads(group, 1)
+            key_terms(group)
+            core_copy(xb, group).start()
 
         def block_at(back):
             return lax.rem(x + jnp.where(step == back, 2, jnp.where(step == back + 1, 1, 3)), NX)
 
-        core_copy(xb).start()
         for s in range(3):
             @pl.when(step == s)
             def _():
@@ -542,18 +575,18 @@
         def _():
             home_stage(block_at(2))
 
-        y_stage(xb)
         return carry
 
     lax.fori_loop(0, 4, backward, 0)
 
-    for r in range(ROWS):
-        dqtx[r] = dq[ROWS + r].astype(BF)
+    mine, theirs = jnp.where(is_home, ROWS, 0), jnp.where(is_home, 0, ROWS)
+    for r in range(ROWS):
+        dqtx[r] = dq[theirs + r].astype(BF)
     dq_copy = rc(dqtx, dqrx, f_s.at[4], f_r.at[4], hpart)
     dq_copy.start()
     dq_copy.wait_recv()
     for r in range(ROWS):
-        d_query = (dq[r] + dqrx[r].astype(F32)) * (DH ** -0.5)
+        d_query = (dq[mine + r] + dqrx[r].astype(F32)) * (DH ** -0.5)
         unit_t = split_nn(w[:, 0:128], d_query) + split_nn(w[:, 384:512], dgp[r])
         dgated[r] = unit_t.T
     z_stage(x)
@@ -579,9 +612,13 @@
         def _():
             key_send[t].wait_send()
     for i in range(4):
-        up(i).wait_send()
-        down(i).wait_send()
-        core_copy(i).wait_send()
+        for p in range(2):
+            if goes_up(i, p):
+                up(i, p).wait_send()
+            if goes_down(i, p):
+                down(i, p).wait_send()
+        core_copy(i, 0).wait_send()
+        core_copy(i, 1).wait_send()
         y_copy(i).wait_send()
         for j in range(1, 8):
             z_copy(i, j).wait_send()
@@ -612,13 +649,14 @@
         vm((8, 3, KB, C), BF), vm((8, 3, C, KB), BF), vm((6, C, 512), BF), vm((6, C, T), F32), vm((6, 8, T), F32),
         vm(blk, BF), vm(blk, BF), vm((ROWS, 8, T), F32), vm((ROWS, 8, T), F32), vm((ROWS, 8, T), F32),
         vm((6, 8, T), F32), vm(blk, F32),
-        vm((6, KB, 512), BF), vm((3, KB, C), BF), vm((3, 160, KB), BF), vm((6, C, 512), BF), vm((HEADS, T, KB), F32),
+        vm((6, KB, 512), BF), vm((3, KB, C), BF), vm((3, 160, KB), BF), vm((6, C, 512), BF), vm((KB, 512), F32),
+        vm((HEADS, T, KB), F32),
         vm((6, C, T), F32), vm((6, 2048, C), BF),
         vm((4, 6, 256, C), BF), vm((4, 3, 256, C), BF), vm((4, 3, 256, C), BF), vm((4, 3, 256, C), F32),
         vm((4, 3, 256, C), BF), vm((4, 8, 3, 32, C), BF), vm((4, 3, 32, C), BF), vm(blk, BF), vm(blk, BF), vm(blk, BF),
         vm((3, HEADS, T, KB), BF), vm((3, HEADS, T, KB), BF),
-        dma((4,)), dma((4,)), dma((2,)), dma((2,)), dma((2, 4)), dma((2, 4)), dma((8,)), dma((8,)),
-        dma((2,)), dma((2,)), dma((3,)), dma((3,)), dma((4,)), dma((4,)), dma((4,)), dma((4,)),
+        dma((4,)), dma((4,)), dma((2,)), dma((2,)), dma((2, 4, 2)), dma((2, 4, 2)), dma((8,)), dma((8,)),
+        dma((2,)), dma((2,)), dma((3,)), dma((3,)), dma((4, 2)), dma((4, 2)), dma((4,)), dma((4,)),
         dma((4, 8)), dma((4, 8)), dma((5,)), dma((5,)), dma((4,)), dma((4,)), dma((3,)),
     ]
     v = pl.BlockSpec(memory_space=pltpu.VMEM)

time: 105 us -> 107 us (1.019)
  Pallas kernels: 104 us -> 106 us
    pallas_call x1, Pallas kernels: 101 us -> 104 us  [shards(): pl.pallas_call(kernel, out_shape=shapes, in_specs=[v] * 8, out_specs=(hbm...]
where the time goes in v6:
time: 107 us
  Pallas kernels  106 us (99%)
  between operations  1.28 us (1%)
    pallas_call x1, Pallas kernels, shards(): pl.pallas_call(kernel, out_shape=shapes, in_specs=[v] * 8, out_specs=(hbm...  104 us
    pallas_call x1, Pallas kernels, shards(): pl.pallas_call(norm_back, out_shape=(shapes[0], shapes[0], shapes[2]), in...  2.53 us

profile of v6, /device:TPU:1, one launch (start us, length us, event | category | flops | bytes accessed | tf_op | source)
XLA Modules:
  0.0 107.4 jit_solution(10533110364050230942)
XLA Ops:
  1.3 103.5 %shard_map.103 = (bf16[3,128,128]{2,1,0:T(8,128)(2,1)}, f32[3,128,128]{2,1,0:T(8,128)}, bf16[4,128,512]{2,1,0:T(8,128)(2,1)}) custom-call(s32[1]{0:T(128)S(6)} %copy.11.tok, bf16[3,128,128]{2,1,0:T(8,128)(2,1)} %codes.3, s32[1,3]{1,0:T(1,128)} %bitcast.2, f32[1,128]{1,0:T(1,128)} %bitcast.4, bf16[128,512]{1,0:T(8,128)(2,1)} %w.1, bf16[128,128]{1,0:T(8,128)(2,1)} %wo.1, ...), custom_call_target="tpu_custom_call" | custom-call | flops 8000000000 | bytes 4000000 | tf_op jit(solution)/shard_map/pallas_call | solution.py:670
  104.8 2.5 %shard_map.104 = (bf16[3,128,128]{2,1,0:T(8,128)(2,1)}, bf16[3,128,128]{2,1,0:T(8,128)(2,1)}, bf16[4,128,512]{2,1,0:T(8,128)(2,1)}) custom-call(bf16[3,128,128]{2,1,0:T(8,128)(2,1)} %codes.3, s32[1,3]{1,0:T(1,128)} %bitcast.3, f32[1,128]{1,0:T(1,128)} %bitcast.5, f32[3,128,128]{2,1,0:T(8,128)} %get-tuple-element.6.d_normed, ...), custom_call_target="tpu_custom_call" | custom-call | tf_op jit(solution)/shard_map/pallas_call | solution.py:681

commit v7 on v6

--- a/solution.py
+++ b/solution.py
@@ -59,8 +59,8 @@
     update_hbm, normed_hbm, bias_hbm,
     update, bias_grad,
     wt, wot, nb, gates, dgated, kn, qt, dot, bias_g, bias_t, probs, s_ref, qbd, dos,
-    m_st, l_st, a_st, vals, keys_t, gk, att_loc, st_loc, att_tx, att_rx, st_rx, back_tx, back_rx, stats, dgp,
-    ds_ref, k_ref, vt_ref, gv_ref, acc, turned, dq, kt, rxc, ytx, rxy, rsum, ztx, zrx, htx, frx, dqtx, dqrx, gtx, grx,
+    m_st, l_st, a_st, vals, keys_t, g_n, att_loc, st_loc, att_tx, att_rx, st_rx, back_tx, back_rx, stats, dgp,
+    ds_ref, k_ref, vt_ref, turned, dq, kt, rxc, ytx, rxy, rsum, ztx, zrx, htx, frx, dqtx, dqrx, gtx, grx,
     bx_s, bx_r, ks_s, ks_r, zr_s, zr_r, sb_s, sb_r, pq_s, pq_r, ex_s, ex_r, kc_s, kc_r,
     ky_s, ky_r, zq_s, zq_r, f_s, f_r, g_s, g_r, o_s,
 ):
@@ -167,6 +167,23 @@
 
     qbd[...] = jnp.zeros_like(qbd)
     dos[...] = jnp.zeros_like(dos)
+
+    def spread(dst, src, row):
+        for h in range(HEADS):
+            rows = slice(h * 32, (h + 1) * 32)
+            dst[row, rows, h * 128 : (h + 1) * 128] = src[row, rows, :]
+
+    def key_factors(row):
+        for part, src in enumerate((qbd, dos)):
+            g = nn(w[:, 128 + part * 128 : 256 + part * 128], src[row])
+            for h in range(HEADS):
+                rows = slice(part * 512 + h * 128, part * 512 + (h + 1) * 128)
+                g_n[row, rows, :] = g[:, h * 128 : (h + 1) * 128].T.astype(BF)
+
+    for r in range(ROWS):
+        spread(qbd, qt, yh * ROWS + r)
+        spread(dos, dot, yh * ROWS + r)
+        key_factors(yh * ROWS + r)
     prep(bias, x)
 
     def block(zz, cc=c):
@@ -250,10 +267,6 @@
         vt_ref[r, 64:80, :] = jnp.ones((16, KB), BF)
         vt_ref[r, 144:160, :] = jnp.ones((16, KB), BF)
 
-    def load_q(r, row):
-        for h in range(HEADS):
-            qbd[r, h * 32 : (h + 1) * 32, h * 128 : (h + 1) * 128] = qt[row, h * 32 : (h + 1) * 32, :]
-
     att_copy = rc(att_tx, att_rx, ex_s.at[0], ex_r.at[0], hpart)
     st_copy = rc(set_of(st_loc, 1 - yh), st_rx, ex_s.at[1], ex_r.at[1], hpart)
     back_copy = rc(back_tx, back_rx, ex_s.at[2], ex_r.at[2], hpart)
@@ -299,10 +312,11 @@
         def _():
             rc(set_of(qt, yh), set_of(qt, 1 - yh), pq_s.at[0], pq_r.at[0], hpart).wait_recv()
             d_send.start()
+            for r in range(ROWS):
+                spread(qbd, qt, (1 - yh) * ROWS + r)
 
         for r in range(ROWS):
             row = side * ROWS + r
-            load_q(r, row)
             n = kn[row, pl.ds(pl.multiple_of(xb * KB, KB), KB), :]
             kv = nn(n, w[:, 128:384]).astype(BF)
             kvt = nt(wt[128:384, :], n).astype(BF)
@@ -318,7 +332,7 @@
         def score(t):
             r, hp = items[t]
             cols = slice(hp * 256, hp * 256 + 256)
-            q2 = qbd[r, :, cols]
+            q2 = qbd[side * ROWS + r, :, cols]
             top = None
             for i in range(4):
                 rows = slice(i * 128, (i + 1) * 128)
@@ -395,11 +409,10 @@
         update[r] = nn(wot[...], (gate * attended).astype(BF)).T.astype(BF)
     update_out = pltpu.make_async_copy(update, update_hbm, o_s.at[0])
     update_out.start()
-    for row in range(6):
-        load_q(0, row)
-        gk[row] = nn(w[:, 128:256], qbd[0]).astype(BF)
-
     rc(set_of(dot, yh), set_of(dot, 1 - yh), pq_s.at[1], pq_r.at[1], hpart).wait_recv()
+    for r in range(ROWS):
+        spread(dos, dot, (1 - yh) * ROWS + r)
+        key_factors((1 - yh) * ROWS + r)
     back_copy.wait_recv()
     for r in range(ROWS):
         stats[(1 - yh) * ROWS + r] = back_rx[r]
@@ -411,11 +424,8 @@
     def z_part(zz):
         return pl.ds(pl.multiple_of(zz * 32, 32), 32)
 
-    def core_copy(xb, p):
-        rows = pl.ds((yl if p else 1 - yl) * ROWS, ROWS)
-        return rc(
-            kt.at[rows, core_half(xb, 1 - c)], rxc.at[xb, rows], kc_s.at[xb, p], kc_r.at[xb, p], sib
-        )
+    def core_copy(xb):
+        return rc(kt.at[:, core_half(xb, 1 - c)], rxc.at[xb], kc_s.at[xb], kc_r.at[xb], sib)
 
     def y_copy(xb):
         return rc(ytx.at[xb], rxy.at[xb], ky_s.at[xb], ky_r.at[xb], ypart)
@@ -433,14 +443,13 @@
         )
 
     def y_stage(xb):
-        core_copy(xb, 0).wait_recv()
+        core_copy(xb).wait_recv()
         for r in range(ROWS):
             theirs = (1 - yl) * ROWS + r
             ytx[xb, r] = (kt[theirs, core_half(xb, c), :].astype(F32) + rxc[xb, theirs].astype(F32)).astype(BF)
         y_copy(xb).start()
 
     def z_stage(xb):
-        core_copy(xb, 1).wait_recv()
         y_copy(xb).wait_recv()
         for r in range(ROWS):
             ours = yl * ROWS + r
@@ -501,67 +510,46 @@
 
     def backward(step, carry):
         xb = lax.rem(x + jnp.where(step == 0, 2, jnp.where(step == 1, 1, jnp.where(step == 2, 3, 0))), NX)
-        places = []
+        places, factors, deltas = [], [], []
         for q in range(2 * ROWS):
-            side = 1 - yl if q < ROWS else yl
-            places.append((q, side * 4 + xb, q % ROWS, side * ROWS + q % ROWS))
-
-        deltas = []
-        for q, sx, r, row in places:
+            side = yh if q < ROWS else 1 - yh
+            sx, r, row = side * 4 + xb, q % ROWS, side * ROWS + q % ROWS
+            places.append((q, sx, r, row))
             st = stats[row]
-            f = jnp.exp(m_st[sx, r] - st[0:4, :])
-            dls = f * st[4:8, :]
-            deltas.append([jnp.concatenate([dls[h : h + 1, :], dls[h + 1 : h + 2, :]], axis=1) for h in (0, 2)])
-            for h in range(HEADS):
-                rows = slice(h * 32, (h + 1) * 32)
-                dos[q, rows, h * 128 : (h + 1) * 128] = (
-                    dot[row, rows, :].astype(F32) * f[h : h + 1, :]
-                ).astype(BF)
-            gv_ref[q] = nn(w[:, 256:384], dos[q]).astype(BF)
-
-        def score_grads(group, hp):
+            f, delta = jnp.exp(m_st[sx, r] - st[0:4, :]), st[4:8, :]
+            factors.append([jnp.concatenate([f[h : h + 1, :], f[h + 1 : h + 2, :]], axis=1) for h in (0, 2)])
+            deltas.append([jnp.concatenate([delta[h : h + 1, :], delta[h + 1 : h + 2, :]], axis=1) for h in (0, 2)])
+        for hp in range(2):
             cols = slice(hp * 256, hp * 256 + 256)
+            p_cols = slice(512 + hp * 256, 768 + hp * 256)
             for i in range(4):
                 rows = slice(i * 128, (i + 1) * 128)
-                total = acc[rows, cols] if group else None
-                for q, sx, r, row in places[group * ROWS : group * ROWS + ROWS]:
-                    d_prob = nn(vals[sx, r, rows, :], dos[q, :, cols]) - deltas[q][hp]
-                    d_score = probs[sx, r, rows, cols].astype(F32) * d_prob
+                total = None
+                for q, sx, r, row in places:
+                    d_prob = nn(vals[sx, r, rows, :], dos[row, :, cols]) - deltas[q][hp]
+                    prob = probs[sx, r, rows, cols].astype(F32) * factors[q][hp]
+                    d_score = prob * d_prob
                     total = d_score if total is None else total + d_score
                     ds_ref[q, rows, cols] = d_score.astype(BF)
-                if group:
-                    for j in range(2):
-                        turned[hp * 2 + j, :, rows] = total[:, j * 128 : (j + 1) * 128].T
-                else:
-                    acc[rows, cols] = total
-
-        def query_grads(group, hp):
-            cols = slice(hp * 256, hp * 256 + 256)
-            for q, sx, r, row in places[group * ROWS : group * ROWS + ROWS]:
+                    ds_ref[q, rows, p_cols] = prob.astype(BF)
+                for j in range(2):
+                    turned[hp * 2 + j, :, rows] = total[:, j * 128 : (j + 1) * 128].T
+            for q, sx, r, row in places:
                 d_query = nn(keys_t[sx, r, hp * 64 : hp * 64 + 64, :], ds_ref[q, :, cols])
                 for j in range(2):
                     rows = slice((hp * 2 + j) * 32, (hp * 2 + j + 1) * 32)
                     dq[q, rows, :] = dq[q, rows, :] + d_query[j * 32 : (j + 1) * 32, j * 128 : (j + 1) * 128]
-
-        def key_terms(group):
-            for q, sx, r, row in places[group * ROWS : group * ROWS + ROWS]:
-                kt[row, pl.ds(pl.multiple_of(xb * KB, KB), KB), :] = (
-                    nt(ds_ref[q], gk[row]) + nt(probs[sx, r], gv_ref[q])
+        for q, sx, r, row in places:
+            for i in range(2):
+                rows = slice(i * 256, (i + 1) * 256)
+                kt[row, pl.ds(pl.multiple_of(xb * KB + i * 256, 256), 256), :] = nn(
+                    ds_ref[q, rows, :], g_n[row]
                 ).astype(BF)
-
-        for group in range(2):
-            score_grads(group, 0)
-            query_grads(group, 0)
-            if group:
-                y_stage(xb)
-            score_grads(group, 1)
-            query_grads(group, 1)
-            key_terms(group)
-            core_copy(xb, group).start()
 
         def block_at(back):
             return lax.rem(x + jnp.where(step == back, 2, jnp.where(step == back + 1, 1, 3)), NX)
 
+        core_copy(xb).start()
         for s in range(3):
             @pl.when(step == s)
             def _():
@@ -575,26 +563,26 @@
         def _():
             home_stage(block_at(2))
 
+        y_stage(xb)
         return carry
 
     lax.fori_loop(0, 4, backward, 0)
 
-    mine, theirs = jnp.where(is_home, ROWS, 0), jnp.where(is_home, 0, ROWS)
-    for r in range(ROWS):
-        dqtx[r] = dq[theirs + r].astype(BF)
+    for r in range(ROWS):
+        dqtx[r] = dq[ROWS + r].astype(BF)
     dq_copy = rc(dqtx, dqrx, f_s.at[4], f_r.at[4], hpart)
     dq_copy.start()
     dq_copy.wait_recv()
     for r in range(ROWS):
-        d_query = (dq[mine + r] + dqrx[r].astype(F32)) * (DH ** -0.5)
+        d_query = (dq[r] + dqrx[r].astype(F32)) * (DH ** -0.5)
         unit_t = split_nn(w[:, 0:128], d_query) + split_nn(w[:, 384:512], dgp[r])
         dgated[r] = unit_t.T
     z_stage(x)
+    home_stage(xs[3])
+    home_stage(x)
     bias_stage(3)
     bias_out = pltpu.make_async_copy(bias_grad, bias_hbm, o_s.at[1])
     bias_out.start()
-    home_stage(xs[3])
-    home_stage(x)
     for j in range(4):
         @pl.when(jnp.logical_not(jnp.logical_and(self_home, lax.rem(z, 4) == j)))
         def _():
@@ -617,8 +605,7 @@
                 up(i, p).wait_send()
             if goes_down(i, p):
                 down(i, p).wait_send()
-        core_copy(i, 0).wait_send()
-        core_copy(i, 1).wait_send()
+        core_copy(i).wait_send()
         y_copy(i).wait_send()
         for j in range(1, 8):
             z_copy(i, j).wait_send()
@@ -643,20 +630,20 @@
         vm(blk, BF), vm((HEADS, T, KB), BF),
         vm((512, C), BF), vm((C, C), BF), vm(blk, BF), vm(blk, F32), vm(blk, F32),
         vm((6, 2048, C), BF), vm((6, C, T), BF), vm((6, C, T), BF), vm((3, HEADS, T, KB), BF),
-        vm((4, KB, 512), F32), vm((8, 3, KB, 512), BF), vm((3, KB, 256), F32), vm((3, C, 512), BF),
+        vm((4, KB, 512), F32), vm((8, 3, KB, 512), BF), vm((3, KB, 256), F32), vm((6, C, 512), BF),
         vm((6, C, 512), BF),
         vm((8, 3, HEADS, T), F32), vm((8, 3, HEADS, T), F32), vm((8, 3, C, T), F32),
-        vm((8, 3, KB, C), BF), vm((8, 3, C, KB), BF), vm((6, C, 512), BF), vm((6, C, T), F32), vm((6, 8, T), F32),
+        vm((8, 3, KB, C), BF), vm((8, 3, C, KB), BF), vm((6, 1024, C), BF), vm((6, C, T), F32), vm((6, 8, T), F32),
         vm(blk, BF), vm(blk, BF), vm((ROWS, 8, T), F32), vm((ROWS, 8, T), F32), vm((ROWS, 8, T), F32),
         vm((6, 8, T), F32), vm(blk, F32),
-        vm((6, KB, 512), BF), vm((3, KB, C), BF), vm((3, 160, KB), BF), vm((6, C, 512), BF), vm((KB, 512), F32),
+        vm((6, KB, 1024), BF), vm((3, KB, C), BF), vm((3, 160, KB), BF),
         vm((HEADS, T, KB), F32),
         vm((6, C, T), F32), vm((6, 2048, C), BF),
         vm((4, 6, 256, C), BF), vm((4, 3, 256, C), BF), vm((4, 3, 256, C), BF), vm((4, 3, 256, C), F32),
         vm((4, 3, 256, C), BF), vm((4, 8, 3, 32, C), BF), vm((4, 3, 32, C), BF), vm(blk, BF), vm(blk, BF), vm(blk, BF),
         vm((3, HEADS, T, KB), BF), vm((3, HEADS, T, KB), BF),
         dma((4,)), dma((4,)), dma((2,)), dma((2,)), dma((2, 4, 2)), dma((2, 4, 2)), dma((8,)), dma((8,)),
-        dma((2,)), dma((2,)), dma((3,)), dma((3,)), dma((4, 2)), dma((4, 2)), dma((4,)), dma((4,)),
+        dma((2,)), dma((2,)), dma((3,)), dma((3,)), dma((4,)), dma((4,)), dma((4,)), dma((4,)),
         dma((4, 8)), dma((4, 8)), dma((5,)), dma((5,)), dma((4,)), dma((4,)), dma((3,)),
     ]
     v = pl.BlockSpec(memory_space=pltpu.VMEM)
@@ -674,7 +661,7 @@
         out_specs=(hbm, hbm, hbm),
         scratch_shapes=scratch,
         compiler_params=pltpu.CompilerParams(
-            collective_id=0, has_side_effects=True, vmem_limit_bytes=58 * 1024 * 1024
+            collective_id=0, has_side_effects=True, vmem_limit_bytes=60 * 1024 * 1024
         ),
         cost_estimate=pl.CostEstimate(flops=8_000_000_000, bytes_accessed=4_000_000, transcendentals=6_300_000),
     )(tok, codes, expo, gain, w, wo, bias, ug)

time: 107 us -> 105 us (0.981)
  Pallas kernels: 106 us -> 104 us
    pallas_call x1, Pallas kernels: 104 us -> 101 us  [shards(): pl.pallas_call(kernel, out_shape=shapes, in_specs=[v] * 8, out_specs=(hbm...]
where the time goes in v7:
time: 105 us
  Pallas kernels  104 us (99%)
  between operations  1.28 us (1%)
    pallas_call x1, Pallas kernels, shards(): pl.pallas_call(kernel, out_shape=shapes, in_specs=[v] * 8, out_specs=(hbm...  101 us
    pallas_call x1, Pallas kernels, shards(): pl.pallas_call(norm_back, out_shape=(shapes[0], shapes[0], shapes[2]), in...  2.53 us

profile of v7, /device:TPU:1, one launch (start us, length us, event | category | flops | bytes accessed | tf_op | source)
XLA Modules:
  0.0 105.2 jit_solution(12959523841271775545)
XLA Ops:
  1.3 101.3 %shard_map.103 = (bf16[3,128,128]{2,1,0:T(8,128)(2,1)}, f32[3,128,128]{2,1,0:T(8,128)}, bf16[4,128,512]{2,1,0:T(8,128)(2,1)}) custom-call(s32[1]{0:T(128)S(6)} %copy.11.tok, bf16[3,128,128]{2,1,0:T(8,128)(2,1)} %codes.3, s32[1,3]{1,0:T(1,128)} %bitcast.2, f32[1,128]{1,0:T(1,128)} %bitcast.4, bf16[128,512]{1,0:T(8,128)(2,1)} %w.1, bf16[128,128]{1,0:T(8,128)(2,1)} %wo.1, ...), custom_call_target="tpu_custom_call" | custom-call | flops 8000000000 | bytes 4000000 | tf_op jit(solution)/shard_map/pallas_call | solution.py:657
  102.6 2.5 %shard_map.104 = (bf16[3,128,128]{2,1,0:T(8,128)(2,1)}, bf16[3,128,128]{2,1,0:T(8,128)(2,1)}, bf16[4,128,512]{2,1,0:T(8,128)(2,1)}) custom-call(bf16[3,128,128]{2,1,0:T(8,128)(2,1)} %codes.3, s32[1,3]{1,0:T(1,128)} %bitcast.3, f32[1,128]{1,0:T(1,128)} %bitcast.5, f32[3,128,128]{2,1,0:T(8,128)} %get-tuple-element.6.d_normed, ...), custom_call_target="tpu_custom_call" | custom-call | tf_op jit(solution)/shard_map/pallas_call | solution.py:668

commit v8 on v7

--- a/solution.py
+++ b/solution.py
@@ -259,6 +259,13 @@
     near = jnp.where(even, zb + 3, zb + 1)
     far = jnp.where(even, zb + 1, zb + 3)
 
+    turned_round = zb == xs[2]
+    order = [jnp.where(turned_round, near, zb), jnp.where(turned_round, zb, near), far, zb + 2]
+
+    @pl.when(turned_round)
+    def _():
+        ring_step(1)
+
     def arrive(phase):
         for i in ((0, 1, 7), (2, 6), (3, 5), (4,))[phase]:
             from_sib(i).wait_recv()
@@ -288,12 +295,12 @@
         phase, second = u // 2, lax.rem(u, 2)
         side = lax.rem(jnp.where(phase == 3, 1 - yh, yh) + second, 2)
         xb = lax.rem(
-            jnp.where(phase == 0, zb, jnp.where(phase == 1, near, jnp.where(phase == 2, far, zb + 2))), NX
+            jnp.where(phase == 0, order[0], jnp.where(phase == 1, order[1], jnp.where(phase == 2, far, zb + 2))), NX
         )
         sx = side * 4 + xb
 
         for i in range(4):
-            @pl.when(u == 2 * i)
+            @pl.when(u == (jnp.where(turned_round, 0, 2) if i == 1 else 2 * i))
             def _():
                 arrive(i)
 
@@ -304,7 +311,7 @@
             prep(bias_g.at[2], xs[2])
 
         for i in range(1, 4):
-            @pl.when(u == 2 * i - 1)
+            @pl.when(u == (jnp.where(turned_round, -1, 1) if i == 1 else 2 * i - 1))
             def _():
                 ring_step(i)
 
@@ -427,8 +434,9 @@
     def core_copy(xb):
         return rc(kt.at[:, core_half(xb, 1 - c)], rxc.at[xb], kc_s.at[xb], kc_r.at[xb], sib)
 
-    def y_copy(xb):
-        return rc(ytx.at[xb], rxy.at[xb], ky_s.at[xb], ky_r.at[xb], ypart)
+    def y_copy(xb, p):
+        part = pl.ds(p * 128, 128)
+        return rc(ytx.at[xb, :, part], rxy.at[xb, :, part], ky_s.at[xb, p], ky_r.at[xb, p], ypart)
 
     def z_copy(xb, i):
         return rc(
@@ -442,23 +450,34 @@
             dev(yh_=yl, yl_=yh, z_=2 * xb + c, c_=z // 4),
         )
 
+    def key_part(xb, p):
+        return pl.ds(pl.multiple_of(xb * KB + c * 256 + p * 128, 128), 128)
+
     def y_stage(xb):
         core_copy(xb).wait_recv()
-        for r in range(ROWS):
-            theirs = (1 - yl) * ROWS + r
-            ytx[xb, r] = (kt[theirs, core_half(xb, c), :].astype(F32) + rxc[xb, theirs].astype(F32)).astype(BF)
-        y_copy(xb).start()
+        for p in range(2):
+            part = slice(p * 128, (p + 1) * 128)
+            for r in range(ROWS):
+                theirs = (1 - yl) * ROWS + r
+                ytx[xb, r, part, :] = (
+                    kt[theirs, key_part(xb, p), :].astype(F32) + rxc[xb, theirs, part, :].astype(F32)
+                ).astype(BF)
+            y_copy(xb, p).start()
 
     def z_stage(xb):
-        y_copy(xb).wait_recv()
-        for r in range(ROWS):
-            ours = yl * ROWS + r
-            total = kt[ours, core_half(xb, c), :].astype(F32) + rxc[xb, ours].astype(F32)
-            total = total + rxy[xb, r].astype(F32)
-            rsum[xb, r] = total
-            ztx[xb, r] = total.astype(BF)
-        for i in (4, 3, 5, 2, 6, 1, 7):
-            z_copy(xb, i).start()
+        for p in range(2):
+            part = slice(p * 128, (p + 1) * 128)
+            y_copy(xb, p).wait_recv()
+            for r in range(ROWS):
+                ours = yl * ROWS + r
+                total = kt[ours, key_part(xb, p), :].astype(F32) + rxc[xb, ours, part, :].astype(F32)
+                total = total + rxy[xb, r, part, :].astype(F32)
+                rsum[xb, r, part, :] = total
+                ztx[xb, r, part, :] = total.astype(BF)
+            for i in (4, 3, 5, 2, 6, 1, 7):
+                @pl.when(zs[i] // 4 == p)
+                def _():
+                    z_copy(xb, i).start()
 
     def home_stage(xb):
         total = rsum[xb, :, z_part(z), :]
@@ -572,13 +591,13 @@
         dqtx[r] = dq[ROWS + r].astype(BF)
     dq_copy = rc(dqtx, dqrx, f_s.at[4], f_r.at[4], hpart)
     dq_copy.start()
+    z_stage(x)
+    home_stage(xs[3])
     dq_copy.wait_recv()
     for r in range(ROWS):
         d_query = (dq[r] + dqrx[r].astype(F32)) * (DH ** -0.5)
         unit_t = split_nn(w[:, 0:128], d_query) + split_nn(w[:, 384:512], dgp[r])
         dgated[r] = unit_t.T
-    z_stage(x)
-    home_stage(xs[3])
     home_stage(x)
     bias_stage(3)
     bias_out = pltpu.make_async_copy(bias_grad, bias_hbm, o_s.at[1])
@@ -606,7 +625,8 @@
             if goes_down(i, p):
                 down(i, p).wait_send()
         core_copy(i).wait_send()
-        y_copy(i).wait_send()
+        y_copy(i, 0).wait_send()
+        y_copy(i, 1).wait_send()
         for j in range(1, 8):
             z_copy(i, j).wait_send()
 
@@ -643,7 +663,7 @@
         vm((4, 3, 256, C), BF), vm((4, 8, 3, 32, C), BF), vm((4, 3, 32, C), BF), vm(blk, BF), vm(blk, BF), vm(blk, BF),
         vm((3, HEADS, T, KB), BF), vm((3, HEADS, T, KB), BF),
         dma((4,)), dma((4,)), dma((2,)), dma((2,)), dma((2, 4, 2)), dma((2, 4, 2)), dma((8,)), dma((8,)),
-        dma((2,)), dma((2,)), dma((3,)), dma((3,)), dma((4,)), dma((4,)), dma((4,)), dma((4,)),
+        dma((2,)), dma((2,)), dma((3,)), dma((3,)), dma((4,)), dma((4,)), dma((4, 2)), dma((4, 2)),
         dma((4, 8)), dma((4, 8)), dma((5,)), dma((5,)), dma((4,)), dma((4,)), dma((3,)),
     ]
     v = pl.BlockSpec(memory_space=pltpu.VMEM)

time: 105 us -> 102 us (0.971)
  Pallas kernels: 104 us -> 101 us
    pallas_call x1, Pallas kernels: 101 us -> 98.2 us  [shards(): pl.pallas_call(kernel, out_shape=shapes, in_specs=[v] * 8, out_specs=(hbm...]
where the time goes in v8:
time: 102 us
  Pallas kernels  101 us (99%)
  between operations  1.28 us (1%)
    pallas_call x1, Pallas kernels, shards(): pl.pallas_call(kernel, out_shape=shapes, in_specs=[v] * 8, out_specs=(hbm...  98.2 us
    pallas_call x1, Pallas kernels, shards(): pl.pallas_call(norm_back, out_shape=(shapes[0], shapes[0], shapes[2]), in...  2.53 us

profile of v8, /device:TPU:1, one launch (start us, length us, event | category | flops | bytes accessed | tf_op | source)
XLA Modules:
  0.0 102.1 jit_solution(1303583944419834839)
XLA Ops:
  1.3 98.2 %shard_map.103 = (bf16[3,128,128]{2,1,0:T(8,128)(2,1)}, f32[3,128,128]{2,1,0:T(8,128)}, bf16[4,128,512]{2,1,0:T(8,128)(2,1)}) custom-call(s32[1]{0:T(128)S(6)} %copy.11.tok, bf16[3,128,128]{2,1,0:T(8,128)(2,1)} %codes.3, s32[1,3]{1,0:T(1,128)} %bitcast.2, f32[1,128]{1,0:T(1,128)} %bitcast.4, bf16[128,512]{1,0:T(8,128)(2,1)} %w.1, bf16[128,128]{1,0:T(8,128)(2,1)} %wo.1, ...), custom_call_target="tpu_custom_call" | custom-call | flops 8000000000 | bytes 4000000 | tf_op jit(solution)/shard_map/pallas_call | solution.py:677
  99.5 2.5 %shard_map.104 = (bf16[3,128,128]{2,1,0:T(8,128)(2,1)}, bf16[3,128,128]{2,1,0:T(8,128)(2,1)}, bf16[4,128,512]{2,1,0:T(8,128)(2,1)}) custom-call(bf16[3,128,128]{2,1,0:T(8,128)(2,1)} %codes.3, s32[1,3]{1,0:T(1,128)} %bitcast.3, f32[1,128]{1,0:T(1,128)} %bitcast.5, f32[3,128,128]{2,1,0:T(8,128)} %get-tuple-element.6.d_normed, ...), custom_call_target="tpu_custom_call" | custom-call | tf_op jit(solution)/shard_map/pallas_call | solution.py:688

commit v9 on v8

--- a/solution.py
+++ b/solution.py
@@ -183,8 +183,6 @@
     for r in range(ROWS):
         spread(qbd, qt, yh * ROWS + r)
         spread(dos, dot, yh * ROWS + r)
-        key_factors(yh * ROWS + r)
-    prep(bias, x)
 
     def block(zz, cc=c):
         return kn.at[:, key_at(zz, cc)]
@@ -246,13 +244,16 @@
         up(0, p).start()
         down(0, p).start()
     to_sib(0).start()
+    prep(bias, x)
+    for r in range(ROWS):
+        key_factors(yh * ROWS + r)
     bias_p.wait_recv()
     bias_fp.start()
     bias_m.wait_recv()
     bias_fm.start()
+    ring_step(0)
     prep(bias_g.at[0], xs[3])
     prep(bias_g.at[1], xs[1])
-    ring_step(0)
 
     zb = z // 2
     even = lax.rem(z, 2) == 0

time: 102 us -> 102 us (level)
  no operation moved by 1% of the time
where the time goes in v9:
time: 102 us
  Pallas kernels  100 us (98%)
  between operations  1.28 us (1%)
    pallas_call x1, Pallas kernels, shards(): pl.pallas_call(kernel, out_shape=shapes, in_specs=[v] * 8, out_specs=(hbm...  97.9 us
    pallas_call x1, Pallas kernels, shards(): pl.pallas_call(norm_back, out_shape=(shapes[0], shapes[0], shapes[2]), in...  2.53 us

profile of v9, /device:TPU:1, one launch (start us, length us, event | category | flops | bytes accessed | tf_op | source)
XLA Modules:
  0.0 101.7 jit_solution(11521215853265947740)
XLA Ops:
  1.3 97.9 %shard_map.103 = (bf16[3,128,128]{2,1,0:T(8,128)(2,1)}, f32[3,128,128]{2,1,0:T(8,128)}, bf16[4,128,512]{2,1,0:T(8,128)(2,1)}) custom-call(s32[1]{0:T(128)S(6)} %copy.11.tok, bf16[3,128,128]{2,1,0:T(8,128)(2,1)} %codes.3, s32[1,3]{1,0:T(1,128)} %bitcast.2, f32[1,128]{1,0:T(1,128)} %bitcast.4, bf16[128,512]{1,0:T(8,128)(2,1)} %w.1, bf16[128,128]{1,0:T(8,128)(2,1)} %wo.1, ...), custom_call_target="tpu_custom_call" | custom-call | flops 8000000000 | bytes 4000000 | tf_op jit(solution)/shard_map/pallas_call | solution.py:678
  99.2 2.5 %shard_map.104 = (bf16[3,128,128]{2,1,0:T(8,128)(2,1)}, bf16[3,128,128]{2,1,0:T(8,128)(2,1)}, bf16[4,128,512]{2,1,0:T(8,128)(2,1)}) custom-call(bf16[3,128,128]{2,1,0:T(8,128)(2,1)} %codes.3, s32[1,3]{1,0:T(1,128)} %bitcast.3, f32[1,128]{1,0:T(1,128)} %bitcast.5, f32[3,128,128]{2,1,0:T(8,128)} %get-tuple-element.6.d_normed, ...), custom_call_target="tpu_custom_call" | custom-call | tf_op jit(solution)/shard_map/pallas_call | solution.py:689

commit v10 on v9

--- a/solution.py
+++ b/solution.py
@@ -410,13 +410,6 @@
             back_tx[r, 4 + h : 5 + h, :] = delta
         att_loc[mine] = attended
     back_copy.start()
-    for r in range(ROWS):
-        attended = att_loc[yh * ROWS + r]
-        gate = gates[r]
-        dgp[r] = dgated[r] * attended * gate * (1.0 - gate)
-        update[r] = nn(wot[...], (gate * attended).astype(BF)).T.astype(BF)
-    update_out = pltpu.make_async_copy(update, update_hbm, o_s.at[0])
-    update_out.start()
     rc(set_of(dot, yh), set_of(dot, 1 - yh), pq_s.at[1], pq_r.at[1], hpart).wait_recv()
     for r in range(ROWS):
         spread(dos, dot, (1 - yh) * ROWS + r)
@@ -432,8 +425,11 @@
     def z_part(zz):
         return pl.ds(pl.multiple_of(zz * 32, 32), 32)
 
-    def core_copy(xb):
-        return rc(kt.at[:, core_half(xb, 1 - c)], rxc.at[xb], kc_s.at[xb], kc_r.at[xb], sib)
+    def core_copy(xb, p):
+        rows = pl.ds(sides[p] * ROWS, ROWS)
+        return rc(
+            kt.at[rows, core_half(xb, 1 - c)], rxc.at[xb, rows], kc_s.at[xb, p], kc_r.at[xb, p], sib
+        )
 
     def y_copy(xb, p):
         part = pl.ds(p * 128, 128)
@@ -455,7 +451,8 @@
         return pl.ds(pl.multiple_of(xb * KB + c * 256 + p * 128, 128), 128)
 
     def y_stage(xb):
-        core_copy(xb).wait_recv()
+        core_copy(xb, 0).wait_recv()
+        core_copy(xb, 1).wait_recv()
         for p in range(2):
             part = slice(p * 128, (p + 1) * 128)
             for r in range(ROWS):
@@ -565,11 +562,12 @@
                 kt[row, pl.ds(pl.multiple_of(xb * KB + i * 256, 256), 256), :] = nn(
                     ds_ref[q, rows, :], g_n[row]
                 ).astype(BF)
+            if r == ROWS - 1:
+                core_copy(xb, q // ROWS).start()
 
         def block_at(back):
             return lax.rem(x + jnp.where(step == back, 2, jnp.where(step == back + 1, 1, 3)), NX)
 
-        core_copy(xb).start()
         for s in range(3):
             @pl.when(step == s)
             def _():
@@ -593,6 +591,13 @@
     dq_copy = rc(dqtx, dqrx, f_s.at[4], f_r.at[4], hpart)
     dq_copy.start()
     z_stage(x)
+    for r in range(ROWS):
+        attended = att_loc[yh * ROWS + r]
+        gate = gates[r]
+        dgp[r] = dgated[r] * attended * gate * (1.0 - gate)
+        update[r] = nn(wot[...], (gate * attended).astype(BF)).T.astype(BF)
+    update_out = pltpu.make_async_copy(update, update_hbm, o_s.at[0])
+    update_out.start()
     home_stage(xs[3])
     dq_copy.wait_recv()
     for r in range(ROWS):
@@ -625,7 +630,8 @@
                 up(i, p).wait_send()
             if goes_down(i, p):
                 down(i, p).wait_send()
-        core_copy(i).wait_send()
+        core_copy(i, 0).wait_send()
+        core_copy(i, 1).wait_send()
         y_copy(i, 0).wait_send()
         y_copy(i, 1).wait_send()
         for j in range(1, 8):
@@ -664,7 +670,7 @@
         vm((4, 3, 256, C), BF), vm((4, 8, 3, 32, C), BF), vm((4, 3, 32, C), BF), vm(blk, BF), vm(blk, BF), vm(blk, BF),
         vm((3, HEADS, T, KB), BF), vm((3, HEADS, T, KB), BF),
         dma((4,)), dma((4,)), dma((2,)), dma((2,)), dma((2, 4, 2)), dma((2, 4, 2)), dma((8,)), dma((8,)),
-        dma((2,)), dma((2,)), dma((3,)), dma((3,)), dma((4,)), dma((4,)), dma((4, 2)), dma((4, 2)),
+        dma((2,)), dma((2,)), dma((3,)), dma((3,)), dma((4, 2)), dma((4, 2)), dma((4, 2)), dma((4, 2)),
         dma((4, 8)), dma((4, 8)), dma((5,)), dma((5,)), dma((4,)), dma((4,)), dma((3,)),
     ]
     v = pl.BlockSpec(memory_space=pltpu.VMEM)

time: 102 us -> 102 us (level)
  no operation moved by 1% of the time
where the time goes in v10:
time: 102 us; the launch traced here: 101 us
  Pallas kernels  100 us (98%)
  between operations  1.28 us (1%)
    pallas_call x1, Pallas kernels, shards(): pl.pallas_call(kernel, out_shape=shapes, in_specs=[v] * 8, out_specs=(hbm...  97.7 us
    pallas_call x1, Pallas kernels, shards(): pl.pallas_call(norm_back, out_shape=(shapes[0], shapes[0], shapes[2]), in...  2.53 us

profile of v10, /device:TPU:1, one launch (start us, length us, event | category | flops | bytes accessed | tf_op | source)
XLA Modules:
  0.0 101.5 jit_solution(8186148136210355861)
XLA Ops:
  1.3 97.7 %shard_map.103 = (bf16[3,128,128]{2,1,0:T(8,128)(2,1)}, f32[3,128,128]{2,1,0:T(8,128)}, bf16[4,128,512]{2,1,0:T(8,128)(2,1)}) custom-call(s32[1]{0:T(128)S(6)} %copy.11.tok, bf16[3,128,128]{2,1,0:T(8,128)(2,1)} %codes.3, s32[1,3]{1,0:T(1,128)} %bitcast.2, f32[1,128]{1,0:T(1,128)} %bitcast.4, bf16[128,512]{1,0:T(8,128)(2,1)} %w.1, bf16[128,128]{1,0:T(8,128)(2,1)} %wo.1, ...), custom_call_target="tpu_custom_call" | custom-call | flops 8000000000 | bytes 4000000 | tf_op jit(solution)/shard_map/pallas_call | solution.py:684
  99.0 2.5 %shard_map.104 = (bf16[3,128,128]{2,1,0:T(8,128)(2,1)}, bf16[3,128,128]{2,1,0:T(8,128)(2,1)}, bf16[4,128,512]{2,1,0:T(8,128)(2,1)}) custom-call(bf16[3,128,128]{2,1,0:T(8,128)(2,1)} %codes.3, s32[1,3]{1,0:T(1,128)} %bitcast.3, f32[1,128]{1,0:T(1,128)} %bitcast.5, f32[3,128,128]{2,1,0:T(8,128)} %get-tuple-element.6.d_normed, ...), custom_call_target="tpu_custom_call" | custom-call | tf_op jit(solution)/shard_map/pallas_call | solution.py:695
